TPU v7x, 32 devices: a whole 2x2x4 slice. The times are simulated.
32 devices in a mesh: role: 4 (over y, x), dp: 8 (over z, core).
Axes of the slice: x: 2, y: 2, z: 4, core: 2. Of those that a mesh axis runs over, the one named last changes fastest.
Arguments:
- wavlm_hidden: bfloat16 [16, 512, 1024], P('dp'), may hold values from -6 to 6
- whisper_hidden: bfloat16 [16, 512, 1280], P('dp'), may hold values from -6 to 6
- wavlm_qkv: bfloat16 [1024, 3072], P(None, 'dp'), may hold values from -8 to 8
- whisper_qkv: bfloat16 [1280, 3840], P(None, 'dp'), may hold values from -8 to 8
- wavlm_out: bfloat16 [1024, 1024], replicated, may hold values from -0.1875 to 0.1875
- whisper_out: bfloat16 [1280, 1280], replicated, may hold values from -0.15625 to 0.15625
- frames_valid: int32 [16], replicated, may hold values from 128 to 512, as said below
- slot_clip: int32 [16], replicated, may hold values from 0 to 15, each once
- latent: bfloat16 [2, 8, 128, 512], P(None, 'dp'), may hold values from -6 to 6
- wavlm_head: bfloat16 [512, 1024], replicated, may hold values from -0.25 to 0.25
- whisper_head: bfloat16 [512, 1280], replicated, may hold values from -0.25 to 0.25
Outputs:
- grad_wavlm_head: float32 [512, 1024], replicated
- grad_whisper_head: float32 [512, 1280], replicated
Inputs may be any that keep to these rules, and one draw needn't show every extreme that they name: `frames_valid`: a multiple of 4; some clip has all 512 frames valid. `slot_clip`: every clip stands in exactly one slot.
All inputs are finite; a program needn't handle non-finite values.
Results may differ from a plain program's by a relative error of at most 0.002.
Values may be sent and summed in bfloat16 or wider, within the bound.
A program may use at most 128 MiB of HBM per device.

v0:
```python
import jax
import jax.numpy as jnp
from jax import lax
from jax.sharding import PartitionSpec as P

WAVLM_D = 1024
WHISPER_D = 1280
STU_D = 512
HEAD = 64
FRAMES = 512
POOL = 4
POOLED = 128


epsilon_norm = 1e-05
epsilon_cos = 1e-06


def layer_norm(hidden):
    hidden_f = hidden.astype(jnp.float32)
    centred = hidden_f - jnp.mean(hidden_f, axis=-1, keepdims=True)
    variance = jnp.mean(centred * centred, axis=-1, keepdims=True)
    return (centred * lax.rsqrt(variance + epsilon_norm)).astype(jnp.bfloat16)


def attend_core(hidden, projected, valid_frames, out_weight):
    full_width = hidden.shape[-1]
    head_count = full_width // HEAD
    frame_count = hidden.shape[0]
    query_rows = projected[:, :full_width].reshape(frame_count, head_count, HEAD)
    key_rows = projected[:, full_width : 2 * full_width].reshape(frame_count, head_count, HEAD)
    value_rows = projected[:, 2 * full_width :].reshape(frame_count, head_count, HEAD)
    scores = jnp.einsum(
        "qhd,khd->hqk", query_rows, key_rows, preferred_element_type=jnp.float32
    ) * HEAD ** (-0.5)
    key_mask = jnp.arange(frame_count) < valid_frames
    scores = jnp.where(key_mask[None, None, :], scores, -1e30)
    row_max = jnp.max(scores, axis=-1, keepdims=True)
    raised = jnp.exp(scores - row_max)
    weights = (raised / jnp.sum(raised, axis=-1, keepdims=True)).astype(jnp.bfloat16)
    attended = jnp.einsum("hqk,khd->qhd", weights, value_rows, preferred_element_type=jnp.float32)
    attended = attended.astype(jnp.bfloat16).reshape(frame_count, full_width)
    result = hidden.astype(jnp.float32) + jnp.dot(
        attended, out_weight, preferred_element_type=jnp.float32
    )
    return jnp.mean(result.reshape(frame_count // POOL, POOL, full_width), axis=1).astype(
        jnp.bfloat16
    )


def head_gradient(latent_rows, target_rows, head_weight, row_mask):
    predicted = jnp.dot(latent_rows, head_weight, preferred_element_type=jnp.float32)
    target_f = target_rows.astype(jnp.float32)
    width_scale = 1.0 / target_rows.shape[-1]
    pred_norm = jnp.sqrt(jnp.sum(predicted * predicted, axis=-1) + epsilon_cos)
    target_norm = jnp.sqrt(jnp.sum(target_f * target_f, axis=-1) + epsilon_cos)
    cosine = jnp.sum(predicted * target_f, axis=-1) / (pred_norm * target_norm)
    slope = (cosine / (pred_norm * pred_norm))[:, None] * predicted - target_f / (
        pred_norm * target_norm
    )[:, None]
    slope = slope + (predicted - target_f) * width_scale
    slope = jnp.where(row_mask[:, None], slope, 0.0).astype(jnp.bfloat16)
    return jnp.einsum("nd,nw->dw", latent_rows, slope, preferred_element_type=jnp.float32)


def per_device(
    wavlm_hidden,
    whisper_hidden,
    wavlm_qkv,
    whisper_qkv,
    wavlm_out,
    whisper_out,
    frames_valid,
    slot_clip,
    latent,
    wavlm_head,
    whisper_head,
):
    role_index = lax.axis_index("role")
    column = lax.axis_index("dp")
    dp_count = lax.axis_size("dp")
    clips_here = wavlm_hidden.shape[0]
    owned = latent.shape[1]
    half_index = role_index % 2
    frame_half = role_index // 2
    half_rows = POOLED // 2
    row_start = frame_half * half_rows
    is_wavlm = role_index == 0
    is_whisper = role_index == 1
    valid_here = lax.dynamic_slice_in_dim(frames_valid, column * clips_here, clips_here)
    wavlm_normed = layer_norm(wavlm_hidden).reshape(clips_here * FRAMES, WAVLM_D)
    whisper_normed = layer_norm(whisper_hidden).reshape(clips_here * FRAMES, WHISPER_D)
    wavlm_piece, whisper_piece = lax.all_gather((wavlm_qkv, whisper_qkv), "dp", axis=1, tiled=True)
    wavlm_cols = lax.cond(
        is_wavlm,
        lambda: jnp.dot(wavlm_normed, wavlm_piece, preferred_element_type=jnp.float32),
        lambda: jnp.zeros((wavlm_normed.shape[0], wavlm_piece.shape[1]), jnp.float32),
    )
    whisper_cols = lax.cond(
        is_whisper,
        lambda: jnp.dot(whisper_normed, whisper_piece, preferred_element_type=jnp.float32),
        lambda: jnp.zeros((whisper_normed.shape[0], whisper_piece.shape[1]), jnp.float32),
    )
    wavlm_proj = wavlm_cols.astype(jnp.bfloat16)
    whisper_proj = whisper_cols.astype(jnp.bfloat16)

    def pool_teacher(hidden, projected, out_weight, active):
        full_width = hidden.shape[-1]
        projected = projected.reshape(clips_here, FRAMES, 3 * full_width)

        def run_clip(clip_args):
            return attend_core(clip_args[0], clip_args[1], clip_args[2], out_weight)

        return lax.cond(
            active,
            lambda: lax.map(run_clip, (hidden, projected, valid_here)),
            lambda: jnp.zeros((clips_here, POOLED, full_width), jnp.bfloat16),
        )

    wavlm_pooled = pool_teacher(wavlm_hidden, wavlm_proj, wavlm_out, is_wavlm)
    whisper_pooled = pool_teacher(whisper_hidden, whisper_proj, whisper_out, is_whisper)
    joined = (
        lax.psum(wavlm_pooled.astype(jnp.float32).astype(jnp.bfloat16), "role").astype(jnp.float32),
        lax.psum(whisper_pooled.astype(jnp.float32).astype(jnp.bfloat16), "role").astype(
            jnp.float32
        ),
    )
    wavlm_ready = joined[0].astype(jnp.bfloat16)
    whisper_ready = joined[1].astype(jnp.bfloat16)
    dest_clips = lax.dynamic_slice_in_dim(
        slot_clip, half_index * dp_count * owned, dp_count * owned
    )
    my_clips = lax.dynamic_slice_in_dim(
        slot_clip, half_index * dp_count * owned + column * owned, owned
    )
    spread = (
        lax.all_to_all(wavlm_ready, "dp", split_axis=1, concat_axis=0, tiled=True),
        lax.all_to_all(whisper_ready, "dp", split_axis=1, concat_axis=0, tiled=True),
    )

    def outgoing(shares):
        chosen = jnp.take(shares, dest_clips, axis=0)
        return chosen.reshape(dp_count, owned, shares.shape[1], shares.shape[2])

    arrived = (
        lax.all_to_all(outgoing(spread[0]), "dp", split_axis=0, concat_axis=2, tiled=True),
        lax.all_to_all(outgoing(spread[1]), "dp", split_axis=0, concat_axis=2, tiled=True),
    )
    wavlm_target = arrived[0].reshape(owned, POOLED, WAVLM_D)
    whisper_target = arrived[1].reshape(owned, POOLED, WHISPER_D)
    latent_slots = lax.dynamic_index_in_dim(latent, half_index, 0, keepdims=False)
    latent_rows = lax.dynamic_slice_in_dim(latent_slots, row_start, half_rows, 1).reshape(
        owned * half_rows, STU_D
    )
    wavlm_rows = lax.dynamic_slice_in_dim(wavlm_target, row_start, half_rows, 1).reshape(
        owned * half_rows, WAVLM_D
    )
    whisper_rows = lax.dynamic_slice_in_dim(whisper_target, row_start, half_rows, 1).reshape(
        owned * half_rows, WHISPER_D
    )
    matches = my_clips[:, None] == jnp.arange(frames_valid.shape[0])[None, :]
    slot_valid = jnp.sum(jnp.where(matches, frames_valid[None, :], 0), axis=1) // POOL
    row_mask = ((row_start + jnp.arange(half_rows))[None, :] < slot_valid[:, None]).reshape(-1)
    grad_wavlm = head_gradient(latent_rows, wavlm_rows, wavlm_head, row_mask)
    grad_whisper = head_gradient(latent_rows, whisper_rows, whisper_head, row_mask)
    summed = lax.psum((grad_wavlm, grad_whisper), ("role", "dp"))
    return summed


def solution(mesh):
    in_specs = (
        P("dp", None, None),
        P("dp", None, None),
        P(None, "dp"),
        P(None, "dp"),
        P(),
        P(),
        P(),
        P(),
        P(None, "dp", None, None),
        P(),
        P(),
    )
    out_specs = (P(), P())
    return jax.shard_map(
        per_device, mesh=mesh, in_specs=in_specs, out_specs=out_specs, check_vma=False
    )
```

profile of v0, /device:TPU:0, one launch (start us, length us, event | category | flops | bytes accessed | tf_op | source)
XLA Modules:
  0.0 568.6 jit_solution(2230640605179794132)
XLA Ops:
  18.7 58.2 %all-gather.3.cloned.1.call-done = bf16[1024,3072]{1,0:T(8,128)(2,1)} async-done(((bf16[1024,384]{1,0:T(8,128)(2,1)}), bf16[1024,3072]{1,0:T(8,128)(2,1)}) %all-gather.3.cloned.1.call-update) | async-done | bytes 6291472 | tf_op jit(solution)/shard_map/all_gather | solution.py:93
  76.9 11.3 %conditional.4 = (bf16[2,512,3072]{2,1,0:T(8,128)(2,1)}) conditional(s32[]{:T(128)} %convert_element_type.114, () %tuple.45, (bf16[2,512,1024]{2,1,0:T(8,128)(2,1)S(1)}, bf16[1024,3072]{1,0:T(8,128)(2,1)}) %tuple.46), branch_computations={%region_3.4_spmd, %region_4.5_spmd} | conditional | flops 6445596672 | bytes 14680072 | solution.py:94
  76.9 11.3 %convolution_convert_fusion = bf16[1024,3072]{1,0:T(8,128)(2,1)} fusion(bf16[1024,1024]{1,0:T(8,128)(2,1)S(1)} %bitcast.174, bf16[1024,3072]{1,0:T(8,128)(2,1)} %get-tuple-element.89), kind=kOutput, calls=%fused_computation.2 | convolution fusion | flops 6445596672 | bytes 14680064 | tf_op jit(solution)/shard_map/cond/branch_1_fun/dot_general | solution.py:96
  88.2 75.9 %conditional.5 = (bf16[2,128,1024]{2,1,0:T(8,128)(2,1)}) conditional(s32[]{:T(128)} %convert_element_type.114, () %tuple.44, (bf16[2,512,1024]{2,1,0:T(8,128)(2,1)}, bf16[2,512,3072]{2,1,0:T(8,128)(2,1)}, s32[2]{0:T(128)}, bf16[1024,1024]{1,0:T(8,128)(2,1)}) %tuple.47), branch_computations={%region_5.6_spmd, %region_6.12_spmd} | conditional | flops 2174878720 | bytes 87361336 | solution.py:114
  88.2 75.9 %while.18 = (s32[]{:T(128)}, bf16[2,128,1024]{2,1,0:T(8,128)(2,1)}, bf16[2,512,1024]{2,1,0:T(8,128)(2,1)}, bf16[2,512,3072]{2,1,0:T(8,128)(2,1)}, s32[2]{0:T(128...) while((s32[]{:T(128)}, bf16[2,128,1024]{2,1,0:T(8,128)(2,1)}, bf16[2,512,1024]{2,1,0:T(8,128)(2,1)}, ...), condition=%wide.region_11.11_spmd, body=%wide.region_7.10_spmd.sunk | while | flops 2174878720 | bytes 87361256 | solution.py:116
  88.2 3.8 constant_dynamic-slice_fusion.5
  91.9 4.7 copy.53
  101.1 10.9 %fusion.144 = (f32[16,512]{1,0:T(8,128)S(1)}, f32[16,512,512]{1,2,0:T(8,128)}) fusion(pred[512]{0:T(512)(128)(4,1)S(1)} %iota_compare_fusion.5, bf16[512,16,64]{0,2,1:T(8,128)(2,1)} %bitcast.171, bf16[512,16,64]{0,2,1:T(8,128)(2,1)S(1)} %bitcast.170), kind=kOutput, calls=%fused_computation.133.clone.1 | convolution fusion | flops 553648640 | bytes 18907648 | tf_op jit(solution)/shard_map/cond/branch_1_fun/while/body/eval_jaxpr/sub | solution.py:39
  112.0 7.6 %fusion.145 = bf16[16,64,512]{2,1,0:T(8,128)(2,1)S(1)} fusion(bf16[512,16,64]{0,2,1:T(8,128)(2,1)S(1)} %bitcast.169, f32[16,512,512]{1,2,0:T(8,128)} %get-tuple-element.300, f32[16,512]{1,0:T(8,128)S(1)} %get-tuple-element.301), kind=kOutput, calls=%fused_computation.14.clone.1 | convolution fusion | flops 545783808 | bytes 18907136 | tf_op jit(solution)/shard_map/cond/branch_1_fun/while/body/eval_jaxpr/hqk,khd->qhd/dot_general | solution.py:41
  126.2 3.8 constant_dynamic-slice_fusion.5
  129.9 4.7 copy.53
  139.0 10.9 %fusion.144 = (f32[16,512]{1,0:T(8,128)S(1)}, f32[16,512,512]{1,2,0:T(8,128)}) fusion(pred[512]{0:T(512)(128)(4,1)S(1)} %iota_compare_fusion.5, bf16[512,16,64]{0,2,1:T(8,128)(2,1)} %bitcast.171, bf16[512,16,64]{0,2,1:T(8,128)(2,1)S(1)} %bitcast.170), kind=kOutput, calls=%fused_computation.133.clone.1 | convolution fusion | flops 553648640 | bytes 18907648 | tf_op jit(solution)/shard_map/cond/branch_1_fun/while/body/eval_jaxpr/sub | solution.py:39
  150.0 7.6 %fusion.145 = bf16[16,64,512]{2,1,0:T(8,128)(2,1)S(1)} fusion(bf16[512,16,64]{0,2,1:T(8,128)(2,1)S(1)} %bitcast.169, f32[16,512,512]{1,2,0:T(8,128)} %get-tuple-element.300, f32[16,512]{1,0:T(8,128)S(1)} %get-tuple-element.301), kind=kOutput, calls=%fused_computation.14.clone.1 | convolution fusion | flops 545783808 | bytes 18907136 | tf_op jit(solution)/shard_map/cond/branch_1_fun/while/body/eval_jaxpr/hqk,khd->qhd/dot_general | solution.py:41
  166.5 4.6 all-gather.5.cloned.1.call-done
  171.2 3.6 conditional.6
  171.2 3.6 reshape.214
  178.3 163.7 %all-reduce.7.cloned.1.call-done = (bf16[2,128,1024]{2,0,1:T(2,128)(2,1)}, bf16[2,128,1280]{2,0,1:T(2,128)(2,1)}) async-done(((bf16[2,128,1024]{2,0,1:T(2,128)(2,1)}, bf16[2,128,1280]{2,0,1:T(2,128)(2,1)}), (bf16[2,128,1024]{2,0,1:T(2,128)(2,1)}, bf16[2,128,1280]{2,0,1:T(2,128)(2,1)})) %all-reduce.7.cloned.1.call-update) | async-done | bytes 1179664 | tf_op jit(solution)/shard_map/psum | solution.py:123
  342.0 20.0 %all_to_all.54 = bf16[2,128,1024]{2,0,1:T(2,128)(2,1)S(1)} all-to-all(bf16[2,128,1024]{2,0,1:T(2,128)(2,1)} %get-tuple-element.188), channel_id=1, replica_groups=mesh['role'=4,'dp'=8] {'dp'}, dimensions={1} | all-to-all | bytes 1048576 | tf_op jit(solution)/shard_map/all_to_all | solution.py:137
  362.0 3.5 all-to-all-start.2
  371.8 11.9 %all-to-all-done.2 = bf16[2,128,1280]{2,0,1:T(2,128)(2,1)S(1)} async-done(((bf16[2,128,1280]{2,0,1:T(2,128)(2,1)}), bf16[2,128,1280]{2,0,1:T(2,128)(2,1)S(1)}, u32[]{:S(2)}, u32[]{:S(2)}) %all-to-all-start.2) | async-done | bytes 655392 | tf_op jit(solution)/shard_map/all_to_all | solution.py:138
  383.6 4.0 all-to-all-start.1
  389.2 8.2 %all-to-all-done.1 = bf16[8,1,16,1024]{3,2,1,0:T(8,128)(2,1)} async-done(((bf16[8,1,16,1024]{3,2,1,0:T(8,128)(2,1)}), bf16[8,1,16,1024]{3,2,1,0:T(8,128)(2,1)}, u32[]{:S(2)}, u32[]{:S(2)}) %all-to-all-start.1) | async-done | bytes 262176 | tf_op jit(solution)/shard_map/all_to_all | solution.py:146
  405.2 6.8 %all-to-all-done.3 = bf16[8,1,16,1280]{3,2,1,0:T(8,128)(2,1)S(1)} async-done(((bf16[8,1,16,1280]{3,2,1,0:T(8,128)(2,1)}), bf16[8,1,16,1280]{3,2,1,0:T(8,128)(2,1)S(1)}, u32[]{:S(2)}, u32[]{:S(2)}) %all-to-all-start.3) | async-done | bytes 327712 | tf_op jit(solution)/shard_map/all_to_all | solution.py:147
  414.6 142.7 %all-reduce.5.cloned.1.call-done = (f32[512,1024]{1,0:T(8,128)}, f32[512,1280]{1,0:T(8,128)}) async-done(((f32[512,1024]{1,0:T(8,128)}, f32[512,1280]{1,0:T(8,128)}), (f32[512,1024]{1,0:T(8,128)}, f32[512,1280]{1,0:T(8,128)})) %all-reduce.5.cloned.1.call-update) | async-done | bytes 4718608 | tf_op jit(solution)/shard_map/psum | solution.py:166
  (88 shorter events, 60.2 us)
Async XLA Ops:
  7.2 404.8 %copy-start = (bf16[512,1280]{1,0:T(8,128)(2,1)S(1)}, bf16[512,1280]{1,0:T(8,128)(2,1)}, u32[]{:S(2)}) copy-start(bf16[512,1280]{1,0:T(8,128)(2,1)} %param.33) | copy-start | bytes 3932164
  7.2 69.7 %all-gather.3.cloned.1.call-start = ((), (), s32[]{:S(2)}) async-start(), calls=%async_computation.4 | async-start | bytes 7077888 | tf_op jit(solution)/shard_map/all_gather | solution.py:93
  7.9 163.2 %all-gather.5.cloned.1.call-start = ((), (), s32[]{:S(2)}) async-start(), calls=%async_computation.5 | async-start | bytes 11059200 | tf_op jit(solution)/shard_map/all_gather | solution.py:93
  8.7 333.4 %all-reduce.7.cloned.1.call-start = ((), (), s32[]{:S(2)}) async-start(), calls=%async_computation.7 | async-start | bytes 2359296 | tf_op jit(solution)/shard_map/psum | solution.py:123
  8.7 5.7 %copy-start.2 = (bf16[2,512,1280]{2,1,0:T(8,128)(2,1)S(1)}, bf16[2,512,1280]{2,1,0:T(8,128)(2,1)}, u32[]{:S(2)}) copy-start(bf16[2,512,1280]{2,1,0:T(8,128)(2,1)} %param.24) | copy-start | bytes 7864324
  10.2 5.1 copy-start.4
  96.6 3.2 copy-start.12
  112.0 7.6 %copy-start.5 = (bf16[2,512,1024]{2,1,0:T(8,128)(2,1)S(1)}, bf16[2,512,1024]{2,1,0:T(8,128)(2,1)}, u32[]{:S(2)}) copy-start(bf16[2,512,1024]{2,1,0:T(8,128)(2,1)} %get-tuple-element.344) | copy-start | bytes 6291460 | tf_op jit(solution)/shard_map/cond/branch_1_fun/while
  112.0 7.6 %copy-start.6 = (bf16[1024,1024]{1,0:T(8,128)(2,1)S(1)}, bf16[1024,1024]{1,0:T(8,128)(2,1)}, u32[]{:S(2)}) copy-start(bf16[1024,1024]{1,0:T(8,128)(2,1)} %get-tuple-element.347) | copy-start | bytes 6291460 | tf_op jit(solution)/shard_map/cond/branch_1_fun/while
  134.7 3.1 copy-start.12
  150.0 7.6 %copy-start.5 = (bf16[2,512,1024]{2,1,0:T(8,128)(2,1)S(1)}, bf16[2,512,1024]{2,1,0:T(8,128)(2,1)}, u32[]{:S(2)}) copy-start(bf16[2,512,1024]{2,1,0:T(8,128)(2,1)} %get-tuple-element.344) | copy-start | bytes 6291460 | tf_op jit(solution)/shard_map/cond/branch_1_fun/while
  150.0 7.6 %copy-start.6 = (bf16[1024,1024]{1,0:T(8,128)(2,1)S(1)}, bf16[1024,1024]{1,0:T(8,128)(2,1)}, u32[]{:S(2)}) copy-start(bf16[1024,1024]{1,0:T(8,128)(2,1)} %get-tuple-element.347) | copy-start | bytes 6291460 | tf_op jit(solution)/shard_map/cond/branch_1_fun/while
  175.7 189.9 %copy-start.10 = (s32[16]{0:T(128)S(1)}, s32[16]{0:T(128)}, u32[]{:S(2)}) copy-start(s32[16]{0:T(128)} %param.30) | copy-start | bytes 196
  175.7 190.5 %copy-start.11 = (s32[16]{0:T(128)S(1)}, s32[16]{0:T(128)}, u32[]{:S(2)}) copy-start(s32[16]{0:T(128)} %param.29) | copy-start | bytes 196
  362.0 21.6 %all-to-all-start.2 = ((bf16[2,128,1280]{2,0,1:T(2,128)(2,1)}), bf16[2,128,1280]{2,0,1:T(2,128)(2,1)S(1)}, u32[]{:S(2)}, u32[]{:S(2)}) async-start(bf16[2,128,1280]{2,0,1:T(2,128)(2,1)} %get-tuple-element.189), calls=%async_computation.2 | async-start | bytes 1310720 | tf_op jit(solution)/shard_map/all_to_all | solution.py:138
  371.8 29.2 %copy-start.8 = (bf16[512,1024]{1,0:T(8,128)(2,1)S(1)}, bf16[512,1024]{1,0:T(8,128)(2,1)}, u32[]{:S(2)}) copy-start(bf16[512,1024]{1,0:T(8,128)(2,1)} %param.32) | copy-start | bytes 3145732
  383.6 13.8 %all-to-all-start.1 = ((bf16[8,1,16,1024]{3,2,1,0:T(8,128)(2,1)}), bf16[8,1,16,1024]{3,2,1,0:T(8,128)(2,1)}, u32[]{:S(2)}, u32[]{:S(2)}) async-start(bf16[8,1,16,1024]{3,2,1,0:T(8,128)(2,1)} %fusion.48), calls=%async_computation.1 | async-start | bytes 524288 | tf_op jit(solution)/shard_map/all_to_all | solution.py:146
  389.2 22.7 %copy-start.9 = (bf16[2,1,128,512]{3,2,1,0:T(8,128)(2,1)S(1)}, bf16[2,1,128,512]{3,2,1,0:T(8,128)(2,1)}, u32[]{:S(2)}) copy-start(bf16[2,1,128,512]{3,2,1,0:T(8,128)(2,1)} %param.31) | copy-start | bytes 786436
  397.4 14.5 %all-to-all-start.3 = ((bf16[8,1,16,1280]{3,2,1,0:T(8,128)(2,1)}), bf16[8,1,16,1280]{3,2,1,0:T(8,128)(2,1)S(1)}, u32[]{:S(2)}, u32[]{:S(2)}) async-start(bf16[8,1,16,1280]{3,2,1,0:T(8,128)(2,1)} %fusion.40), calls=%async_computation.3 | async-start | bytes 655360 | tf_op jit(solution)/shard_map/all_to_all | solution.py:147
  400.9 156.4 %all-reduce.5.cloned.1.call-start = ((), (), s32[]{:S(2)}) async-start(), calls=%async_computation.6 | async-start | bytes 9437184 | tf_op jit(solution)/shard_map/psum | solution.py:166
  557.3 3.3 copy-start.7
Sparse Core Ops, SparseCore 0:
  9.6 67.2 all-gather.2
  78.5 92.5 all-gather.4
  178.4 163.5 all-reduce.6
  414.7 142.5 all-reduce.4
where the time goes:
time: 570 us; the launch traced here: 569 us
  waiting for transfers between devices  398 us (70%)
  matrix products  57.6 us (10%)
  local copies, waits for them, and re-layouts  45.6 us (8%)
  other arithmetic  20 us (4%)
  blocking collectives  20 us (4%)
  between operations  16.6 us (3%)
  starting transfers between devices  11.2 us (2%)
    psum x1, waiting for transfers between devices, per_device(): lax.psum(wavlm_pooled.astype(jnp.float32).astype(jnp.bfloat16), 'role')  164 us
    psum x1, waiting for transfers between devices, per_device(): summed = lax.psum((grad_wavlm, grad_whisper), ('role', 'dp'))  143 us
    all_gather x2, waiting for transfers between devices, per_device(): lax.all_gather((wavlm_qkv, whisper_qkv), 'dp', axis=1, tiled=True)  62.8 us
    sub x2, matrix products, attend_core(): raised = jnp.exp(scores - row_max)  21.8 us
    all_to_all x1, blocking collectives, per_device(): lax.all_to_all(wavlm_ready, 'dp', split_axis=1, concat_axis=0, tiled=True)  20 us
    dynamic_slice x6, local copies, waits for them, and re-layouts, pool_teacher(): lax.map(run_clip, (hidden, projected, valid_here))  18.2 us
    dot_general x2, matrix products, attend_core(): jnp.einsum('hqk,khd->qhd', weights, value_rows, preferred_element_type=jn...  15.2 us
    all_to_all x1, waiting for transfers between devices, per_device(): lax.all_to_all(whisper_ready, 'dp', split_axis=1, concat_axis=0, tiled=True)  11.9 us
  transfers between devices with their start and end apart: 7, of which 7 were waited for; matrix products, arithmetic and copies ran while one was open for 19% of the time, Pallas kernels for 0%

commit v1 on v0

v1 whole, which is shorter than its diff:
```python
import functools

import numpy as np

import jax
import jax.numpy as jnp
from jax import lax
from jax.experimental import pallas as pl
from jax.experimental.pallas import tpu as pltpu
from jax.sharding import PartitionSpec as P

HEAD = 64
POOL = 4
LOG2E = 1.4426950408889634

epsilon_norm = 1e-05
epsilon_cos = 1e-06


def column_tables(width, shards, roles):
    total = 3 * width
    per_shard = total // shards
    column = np.arange(total)
    role_of = ((column % width) // HEAD) % roles
    counts = [
        np.sum(role_of[s * per_shard : (s + 1) * per_shard] == r)
        for r in range(roles)
        for s in range(shards)
    ]
    slots = -(-int(max(counts)) // HEAD) * HEAD
    send = np.full((roles, shards, slots), -1, np.int32)
    where = np.zeros(total, np.int32)
    for r in range(roles):
        for s in range(shards):
            local = np.nonzero(role_of[s * per_shard : (s + 1) * per_shard] == r)[0]
            send[r, s, : local.size] = local
            where[s * per_shard + local] = s * slots + np.arange(local.size)
    receive = np.stack([where[role_of == r] for r in range(roles)])
    return send, receive.astype(np.int32)


def teacher_kernel(valid_ref, table_ref, hidden_ref, gathered_ref, out_ref, weight, projected, attended):
    clip = pl.program_id(0)
    width, columns = gathered_ref.shape
    needed = weight.shape[1]
    mine = needed // 3
    frames = hidden_ref.shape[1]
    rows = 128

    @pl.when(clip == 0)
    def _():
        place = lax.broadcasted_iota(jnp.int32, (columns, needed), 0) == table_ref[...]
        place = place.astype(jnp.float32).astype(jnp.bfloat16)

        @pl.loop(0, width // 256)
        def _(i):
            part = pl.ds(pl.multiple_of(i * 256, 256), 256)
            weight[part, :] = jnp.dot(
                gathered_ref[part, :], place, preferred_element_type=jnp.float32
            ).astype(jnp.bfloat16)

    @pl.loop(0, frames // rows)
    def _(i):
        part = pl.ds(pl.multiple_of(i * rows, rows), rows)
        hidden = hidden_ref[0, part, :].astype(jnp.float32)
        centred = hidden - jnp.mean(hidden, axis=-1, keepdims=True)
        variance = jnp.mean(centred * centred, axis=-1, keepdims=True)
        normed = (centred * lax.rsqrt(variance + epsilon_norm)).astype(jnp.bfloat16)
        projected[part, :] = jnp.dot(
            normed, weight[...], preferred_element_type=jnp.float32
        ).astype(jnp.bfloat16)

    key_index = lax.broadcasted_iota(jnp.int32, (1, frames), 1)
    bias = jnp.where(key_index < valid_ref[clip], 0.0, -1e30)
    ones = jnp.ones((frames, HEAD), jnp.bfloat16)
    scale = HEAD ** (-0.5) * LOG2E
    half = 256
    for j in range(mine // HEAD):
        lanes = slice(j * HEAD, (j + 1) * HEAD)
        keys = projected[:, mine + j * HEAD : mine + (j + 1) * HEAD]
        values = projected[:, 2 * mine + j * HEAD : 2 * mine + (j + 1) * HEAD]
        values = jnp.concatenate([values, ones], axis=1)
        for h in range(frames // half):
            query = projected[h * half : (h + 1) * half, lanes]
            scores = lax.dot_general(
                query, keys, (((1,), (1,)), ((), ())), preferred_element_type=jnp.float32
            )
            scores = scores + bias
            top = jnp.max(scores, axis=-1, keepdims=True)
            raised = jnp.exp2((scores - top) * scale).astype(jnp.bfloat16)
            both = jnp.dot(raised, values, preferred_element_type=jnp.float32)
            attended[h * half : (h + 1) * half, lanes] = (
                both[:, :HEAD] / both[:, HEAD : HEAD + 1]
            ).astype(jnp.bfloat16)

    pooled = frames // POOL
    row = lax.broadcasted_iota(jnp.int32, (pooled, frames), 0)
    column = lax.broadcasted_iota(jnp.int32, (pooled, frames), 1)
    average = jnp.where(column // POOL == row, 1.0 / POOL, 0.0).astype(jnp.bfloat16)
    out_ref[0] = jnp.dot(average, attended[...], preferred_element_type=jnp.float32).astype(
        jnp.bfloat16
    )


def teacher(hidden, gathered, table, valid):
    clips, frames, width = hidden.shape
    columns = gathered.shape[1]
    needed = table.shape[1]
    mine = needed // 3
    return pl.pallas_call(
        teacher_kernel,
        grid=(clips,),
        out_shape=jax.ShapeDtypeStruct((clips, frames // POOL, mine), jnp.bfloat16),
        in_specs=[
            pl.BlockSpec(memory_space=pltpu.SMEM),
            pl.BlockSpec((1, needed), lambda i: (0, 0)),
            pl.BlockSpec((1, frames, width), lambda i: (i, 0, 0)),
            pl.BlockSpec((width, columns), lambda i: (0, 0)),
        ],
        out_specs=pl.BlockSpec((1, frames // POOL, mine), lambda i: (i, 0, 0)),
        scratch_shapes=[
            pltpu.VMEM((width, needed), jnp.bfloat16),
            pltpu.VMEM((frames, needed), jnp.bfloat16),
            pltpu.VMEM((frames, mine), jnp.bfloat16),
        ],
        compiler_params=pltpu.CompilerParams(vmem_limit_bytes=40 * 1024 * 1024),
        cost_estimate=pl.CostEstimate(
            flops=2 * clips * frames * needed * (width + frames),
            bytes_accessed=2 * width * (columns + clips * frames),
            transcendentals=clips * frames * frames * mine // HEAD,
        ),
    )(valid, table, hidden, gathered)


def slope_of(latent_rows, target, head_weight, row_mask):
    predicted = jnp.dot(latent_rows, head_weight, preferred_element_type=jnp.float32)
    target_f = target.astype(jnp.float32)
    width_scale = 1.0 / target.shape[-1]
    pred_norm = jnp.sqrt(jnp.sum(predicted * predicted, axis=-1) + epsilon_cos)
    target_norm = jnp.sqrt(jnp.sum(target_f * target_f, axis=-1) + epsilon_cos)
    cosine = jnp.sum(predicted * target_f, axis=-1) / (pred_norm * target_norm)
    slope = (cosine / (pred_norm * pred_norm))[:, None] * predicted - target_f / (
        pred_norm * target_norm
    )[:, None]
    slope = slope + (predicted - target_f) * width_scale
    return jnp.where(row_mask[:, None], slope, 0.0).astype(jnp.bfloat16)


def per_device(
    wavlm_hidden,
    whisper_hidden,
    wavlm_qkv,
    whisper_qkv,
    wavlm_out,
    whisper_out,
    frames_valid,
    slot_clip,
    latent,
    wavlm_head,
    whisper_head,
):
    role = lax.axis_index("role")
    column = lax.axis_index("dp")
    roles = lax.axis_size("role")
    dp_count = lax.axis_size("dp")
    devices = roles * dp_count
    clips_here, frames = wavlm_hidden.shape[:2]
    pooled = frames // POOL
    quarter = pooled // roles
    stu = latent.shape[-1]
    all_clips = frames_valid.shape[0]
    valid_here = lax.dynamic_slice_in_dim(frames_valid, column * clips_here, clips_here)

    def my_columns(shard, width):
        send, receive = column_tables(width, dp_count, roles)
        wanted = jnp.asarray(send)[role, column]
        place = jnp.arange(shard.shape[1])[:, None] == wanted[None, :]
        picked = jnp.dot(shard, place.astype(jnp.bfloat16), preferred_element_type=jnp.float32)
        return picked.astype(jnp.bfloat16), jnp.asarray(receive)[role][None, :]

    wavlm_width = wavlm_hidden.shape[-1]
    whisper_width = whisper_hidden.shape[-1]
    wavlm_part, wavlm_table = my_columns(wavlm_qkv, wavlm_width)
    whisper_part, whisper_table = my_columns(whisper_qkv, whisper_width)
    wavlm_all, whisper_all, latent_all = lax.all_gather(
        (wavlm_part, whisper_part, latent), "dp", axis=1, tiled=True
    )

    wavlm_att = teacher(wavlm_hidden, wavlm_all, wavlm_table, valid_here)
    whisper_att = teacher(whisper_hidden, whisper_all, whisper_table, valid_here)
    att = jnp.concatenate([wavlm_att, whisper_att], axis=-1)
    mine = att.shape[-1]
    att = att.reshape(clips_here, roles, quarter, mine).transpose(1, 0, 2, 3)
    att = lax.all_to_all(att, "role", split_axis=0, concat_axis=0, tiled=True)
    att = att.reshape(roles, clips_here * quarter, mine)

    slots = jnp.arange(all_clips)
    slot_of = jnp.sum(jnp.where(slot_clip[None, :] == slots[:, None], slots[None, :], 0), axis=1)
    latent_by_clip = jnp.take(latent_all.reshape(all_clips, pooled, stu), slot_of, axis=0)
    latent_rows = lax.dynamic_slice(
        latent_by_clip, (column * clips_here, role * quarter, 0), (clips_here, quarter, stu)
    ).reshape(clips_here * quarter, stu)
    row_mask = (
        (role * quarter + jnp.arange(quarter))[None, :] < (valid_here // POOL)[:, None]
    ).reshape(-1)

    def slope_teacher(hidden, att_rows, out_weight, head_weight):
        width = hidden.shape[-1]
        here = lax.dynamic_slice_in_dim(hidden, role * quarter * POOL, quarter * POOL, 1)
        here = jnp.mean(
            here.astype(jnp.float32).reshape(clips_here * quarter, POOL, width), axis=1
        )
        weight = out_weight.reshape(-1, roles, HEAD, width).transpose(1, 0, 2, 3)
        weight = weight.reshape(width, width)
        rows = att_rows.transpose(1, 0, 2).reshape(clips_here * quarter, width)
        target = here + jnp.dot(rows, weight, preferred_element_type=jnp.float32)
        return slope_of(latent_rows, target.astype(jnp.bfloat16), head_weight, row_mask)

    split = wavlm_att.shape[-1]
    slope = jnp.concatenate(
        [
            slope_teacher(wavlm_hidden, att[:, :, :split], wavlm_out, wavlm_head),
            slope_teacher(whisper_hidden, att[:, :, split:], whisper_out, whisper_head),
        ],
        axis=1,
    )
    block = slope.shape[1] // devices
    slope = slope.reshape(-1, devices, block).transpose(1, 0, 2)
    slope = lax.all_to_all(slope, ("role", "dp"), split_axis=0, concat_axis=0, tiled=True)
    slope = slope.reshape(roles, dp_count, clips_here, quarter, block).transpose(1, 2, 0, 3, 4)
    slope = slope.reshape(all_clips * pooled, block)
    grad = lax.dot_general(
        slope,
        latent_by_clip.reshape(all_clips * pooled, stu),
        (((0,), (0,)), ((), ())),
        preferred_element_type=jnp.float32,
    )
    grad = lax.all_gather(grad, ("role", "dp"), axis=0, tiled=True)
    return grad[:wavlm_width].T, grad[wavlm_width:].T


def solution(mesh):
    in_specs = (
        P("dp", None, None),
        P("dp", None, None),
        P(None, "dp"),
        P(None, "dp"),
        P(),
        P(),
        P(),
        P(),
        P(None, "dp", None, None),
        P(),
        P(),
    )
    out_specs = (P(), P())
    return jax.shard_map(
        per_device, mesh=mesh, in_specs=in_specs, out_specs=out_specs, check_vma=False
    )
```

time: 570 us -> 258 us (0.45)
  waiting for transfers between devices: 398 us -> 120 us
  matrix products: 57.6 us -> 10.8 us
  Pallas kernels: 0 us -> 32.8 us
  other arithmetic: 20 us -> 12.7 us
  starting transfers between devices: 11.2 us -> 4.44 us
    psum x2 -> x0, waiting for transfers between devices: 306 us -> none  [the longest x1 164 us: per_device(): lax.psum(wavlm_pooled.astype(jnp.float32).astype(jnp.bfloat16), 'role')]
    all_gather x2 -> x4, waiting for transfers between devices: 62.8 us -> 115 us  [the longest x1 61.4 us: per_device(): grad = lax.all_gather(grad, ('role', 'dp'), axis=0, tiled=True)]
    pallas_call x0 -> x2, Pallas kernels: none -> 32.8 us  [teacher(): pl.pallas_call(teacher_kernel, grid=(clips,), out_shape=jax.ShapeDtypeStr...]
    dot_general x9 -> x7, matrix products: 35.8 us -> 10.8 us  [the longest x2 4.91 us: my_columns(): jnp.dot(shard, place.astype(jnp.bfloat16), preferred_element_type=jnp.flo...]
    all_to_all x3 -> x1, waiting for transfers between devices: 26.9 us -> 4.52 us  [per_device(): att = lax.all_to_all(att, 'role', split_axis=0, concat_axis=0, tiled=True)]
    sub x2 -> x0, matrix products: 21.8 us -> none  [attend_core(): raised = jnp.exp(scores - row_max)]
    dynamic_slice x8 -> x3, local copies, waits for them, and re-layouts: 20.3 us -> 1.45 us  [the longest x2 1.44 us: my_columns(): return (picked.astype(jnp.bfloat16), jnp.asarray(receive)[role][None, :])]
    transpose x0 -> x7, local copies, waits for them, and re-layouts: none -> 12.4 us  [the longest x2 5.3 us: slope_teacher(): weight = out_weight.reshape(-1, roles, HEAD, width).transpose(1, 0, 2, 3)]
  transfers between devices with their start and end apart: 7 -> 5, of which waited for: 7 -> 5; matrix products, arithmetic and copies ran while one was open for 19% -> 13% of each run, Pallas kernels for 0% -> 6%
where the time goes in v1:
time: 258 us; the launch traced here: 257 us
  waiting for transfers between devices  120 us (47%)
  local copies, waits for them, and re-layouts  43.5 us (17%)
  Pallas kernels  32.8 us (13%)
  blocking collectives  19.2 us (7%)
  between operations  14 us (5%)
  other arithmetic  12.7 us (5%)
  matrix products  10.8 us (4%)
  starting transfers between devices  4.44 us (2%)
    all_gather x1, waiting for transfers between devices, per_device(): grad = lax.all_gather(grad, ('role', 'dp'), axis=0, tiled=True)  61.4 us
    all_gather x3, waiting for transfers between devices, per_device(): lax.all_gather((wavlm_part, whisper_part, latent), 'dp', axis=1, tiled=True)  53.2 us
    pallas_call x2, Pallas kernels, teacher(): pl.pallas_call(teacher_kernel, grid=(clips,), out_shape=jax.ShapeDtypeStr...  32.8 us
    all_to_all x1, blocking collectives, per_device(): lax.all_to_all(slope, ('role', 'dp'), split_axis=0, concat_axis=0, tiled=...  19.2 us
    unnamed x27, local copies, waits for them, and re-layouts  11.7 us
    reduce_sum x2, other arithmetic, slope_teacher(): jnp.mean(here.astype(jnp.float32).reshape(clips_here * quarter, POOL, wid...  5.4 us
    transpose x2, local copies, waits for them, and re-layouts, slope_teacher(): weight = out_weight.reshape(-1, roles, HEAD, width).transpose(1, 0, 2, 3)  5.3 us
    transpose x2, local copies, waits for them, and re-layouts, per_device(): return (grad[:wavlm_width].T, grad[wavlm_width:].T)  5.27 us
  transfers between devices with their start and end apart: 5, of which 5 were waited for; matrix products, arithmetic and copies ran while one was open for 13% of the time, Pallas kernels for 6%

profile of v1, /device:TPU:0, one launch (start us, length us, event | category | flops | bytes accessed | tf_op | source)
XLA Modules:
  0.0 257.4 jit_solution(16215695138293918565)
XLA Ops:
  8.7 2.2 fusion.3
  11.7 2.7 %fusion = bf16[1280,128]{1,0:T(8,128)(2,1)} fusion(bf16[1280,480]{0,1:T(8,128)(2,1)} %param.18, s32[128]{0:T(128)S(1)} %fusion.9), kind=kOutput, calls=%fused_computation.4 | convolution fusion | flops 157511680 | bytes 1556992 | tf_op jit(solution)/shard_map/dot_general | solution.py:178
  15.8 2.5 reshape.182
  18.2 2.2 dynamic-slice_convert_fusion
  20.5 2.6 %reshape.184 = f32[64,4,1280]{2,1,0:T(4,128)} reshape(f32[2,128,1280]{2,1,0:T(8,128)} %dynamic-slice_convert_fusion) | data formatting | bytes 2621440 | tf_op jit(solution)/shard_map/reshape | solution.py:211
  23.1 2.6 reduce_sum.85
  25.7 2.8 %reduce_sum.89 = f32[64,1280]{1,0:T(8,128)} reduce(f32[64,4,1280]{2,1,0:T(4,128)} %reshape.184, f32[]{:T(128)} %constant.66.clone.1), dimensions={1}, to_apply=%region_5.6 | reduce | flops 245760 | bytes 1638404 | tf_op jit(solution)/shard_map/reduce_sum | solution.py:210
  28.5 3.3 %copy.43 = bf16[4,4,64,1024]{3,2,1,0:T(8,128)(2,1)} copy(bf16[4,4,64,1024]{3,2,0,1:T(8,128)(2,1)} %bitcast.61) | data formatting | bytes 4194304 | tf_op jit(solution)/shard_map/transpose | solution.py:213
  31.8 2.0 copy.45
  36.0 5.5 %all-gather.5.cloned.1.call-done = bf16[2,8,128,512]{3,2,1,0:T(8,128)(2,1)} async-done(((bf16[2,1,128,512]{3,2,1,0:T(8,128)(2,1)}), bf16[2,8,128,512]{3,2,1,0:T(8,128)(2,1)}) %all-gather.5.cloned.1.call-update) | async-done | bytes 2097168 | tf_op jit(solution)/shard_map/all_gather | solution.py:185
  41.5 3.6 %gather_fusion = bf16[16,128,512]{2,1,0:T(8,128)(2,1)} fusion(bf16[16,128,512]{2,1,0:T(8,128)(2,1)} %bitcast.62, s32[1024]{0:T(1024)S(1)} %pad_clamp_fusion), kind=kCustom, calls=%fused_computation | custom fusion | bytes 4194368 | tf_op jit(solution)/shard_map/jit(_take)/gather | solution.py:199
  45.1 28.4 %all-gather.7.cloned.1.call-done.gathered_ref = bf16[1024,1024]{1,0:T(8,128)(2,1)} async-done(((bf16[1024,128]{1,0:T(8,128)(2,1)}), bf16[1024,1024]{1,0:T(8,128)(2,1)}) %all-gather.7.cloned.1.call-update) | async-done | bytes 2097168 | tf_op jit(solution)/shard_map/all_gather | solution.py:185
  75.0 14.6 %shard_map.158 = bf16[2,128,256]{2,1,0:T(8,128)(2,1)S(1)} custom-call(s32[2]{0:T(128)S(1)} %get-tuple-element.17.valid_ref, s32[1,768]{1,0:T(1,128)S(1)} %constant_dynamic-slice_fusion.3.table_ref, bf16[2,512,1024]{2,1,0:T(8,128)(2,1)S(1)} %copy-done.2, bf16[1024,1024]{1,0:T(8,128)(2,1)S(1)} %copy-done.4), custom_call_target="tpu_custom_call" | custom-call | flops 2415919104 | bytes 4194304 | tf_op jit(solution)/shard_map/pallas_call | solution.py:110
  89.6 19.4 %all-gather.9.cloned.1.call-done.gathered_ref = bf16[1280,1024]{1,0:T(8,128)(2,1)} async-done(((bf16[1280,128]{1,0:T(8,128)(2,1)}), bf16[1280,1024]{1,0:T(8,128)(2,1)}) %all-gather.9.cloned.1.call-update) | async-done | bytes 2621456 | tf_op jit(solution)/shard_map/all_gather | solution.py:185
  112.5 18.2 %shard_map.159 = bf16[2,128,320]{2,1,0:T(8,128)(2,1)S(1)} custom-call(s32[2]{0:T(128)S(1)} %get-tuple-element.17.valid_ref, s32[1,960]{1,0:T(1,128)S(1)} %constant_dynamic-slice_fusion.1.table_ref, bf16[2,512,1280]{2,1,0:T(8,128)(2,1)S(1)} %copy-done.1, bf16[1280,1024]{1,0:T(8,128)(2,1)S(1)} %copy-done.3), custom_call_target="tpu_custom_call" | custom-call | flops 3523215360 | bytes 5242880 | tf_op jit(solution)/shard_map/pallas_call | solution.py:110
  131.5 4.1 %all-to-all-start = ((bf16[4,2,32,576]{3,2,1,0:T(8,128)(2,1)}), bf16[4,2,32,576]{3,2,1,0:T(8,128)(2,1)}, u32[]{:S(2)}, u32[]{:S(2)}) async-start(bf16[4,2,32,576]{3,2,1,0:T(8,128)(2,1)} %bitcast.56), calls=%async_computation | async-start | bytes 655360 | tf_op jit(solution)/shard_map/all_to_all | solution.py:194
  135.9 1.9 broadcast_select_fusion
  137.7 4.5 %all-to-all-done = bf16[4,2,32,576]{3,2,1,0:T(8,128)(2,1)} async-done(((bf16[4,2,32,576]{3,2,1,0:T(8,128)(2,1)}), bf16[4,2,32,576]{3,2,1,0:T(8,128)(2,1)}, u32[]{:S(2)}, u32[]{:S(2)}) %all-to-all-start) | async-done | bytes 294944 | tf_op jit(solution)/shard_map/all_to_all | solution.py:194
  148.5 2.2 fusion.5
  154.5 2.9 %reshape.178 = bf16[64,32,72]{2,1,0:T(8,128)(2,1)} reshape(bf16[64,2304]{1,0:T(8,128)(2,1)} %pad_maximum_fusion.1) | data formatting | bytes 589824 | tf_op jit(solution)/shard_map/reshape | solution.py:228
  158.7 19.2 %all_to_all.10 = bf16[32,64,72]{2,1,0:T(8,128)(2,1)S(1)} all-to-all(bf16[32,64,72]{2,1,0:T(8,128)(2,1)S(1)} %bitcast.63), channel_id=1, replica_groups=mesh['role'=4,'dp'=8] {'role','dp'}, dimensions={0} | all-to-all | bytes 589824 | tf_op jit(solution)/shard_map/all_to_all | solution.py:229
  179.1 61.4 %all-gather.11.cloned.1.call-done = f32[2304,512]{1,0:T(8,128)} async-done(((f32[72,512]{1,0:T(8,128)}), f32[2304,512]{1,0:T(8,128)}) %all-gather.11.cloned.1.call-update) | async-done | bytes 4718608 | tf_op jit(solution)/shard_map/all_gather | solution.py:238
  240.6 3.5 %slice_bitcast_fusion = f32[512,1280]{0,1:T(8,128)} fusion(f32[2304,512]{1,0:T(8,128)} %all-gather.11.cloned.1.call-done), kind=kLoop, calls=%fused_computation.1 | loop fusion | bytes 5242880 | tf_op jit(solution)/shard_map/transpose | solution.py:239
  244.1 3.2 %copy.49 = f32[512,1280]{1,0:T(8,128)} copy(f32[512,1280]{0,1:T(8,128)} %slice_bitcast_fusion) | data formatting | bytes 5242880
  (66 shorter events, 27.9 us)
Async XLA Ops:
  7.2 145.6 %copy-start = (bf16[512,1280]{1,0:T(8,128)(2,1)S(1)}, bf16[512,1280]{1,0:T(8,128)(2,1)}, u32[]{:S(2)}) copy-start(bf16[512,1280]{1,0:T(8,128)(2,1)} %param.25) | copy-start | bytes 3932164
  7.2 7.2 %copy-start.10 = (s32[16]{0:T(128)S(1)}, s32[16]{0:T(128)}, u32[]{:S(2)}) copy-start(s32[16]{0:T(128)} %param.21) | copy-start | bytes 196
  7.2 7.5 %copy-start.2 = (bf16[2,512,1024]{2,1,0:T(8,128)(2,1)S(1)}, bf16[2,512,1024]{2,1,0:T(8,128)(2,1)}, u32[]{:S(2)}) copy-start(bf16[2,512,1024]{2,1,0:T(8,128)(2,1)} %hidden_ref.2) | copy-start | bytes 6291460
  7.2 34.3 %all-gather.5.cloned.1.call-start = ((), (), s32[]{:S(2)}) async-start(), calls=%async_computation.2 | async-start | bytes 2359296 | tf_op jit(solution)/shard_map/all_gather | solution.py:185
  7.9 65.5 %all-gather.7.cloned.1.call-start = ((), (), s32[]{:S(2)}) async-start(), calls=%async_computation.3 | async-start | bytes 2359296 | tf_op jit(solution)/shard_map/all_gather | solution.py:185
  10.9 98.1 %all-gather.9.cloned.1.call-start = ((), (), s32[]{:S(2)}) async-start(), calls=%async_computation.4 | async-start | bytes 2949120 | tf_op jit(solution)/shard_map/all_gather | solution.py:185
  28.5 3.3 %copy-start.6 = (bf16[1280,1280]{1,0:T(8,128)(2,1)S(1)}, bf16[1280,1280]{1,0:T(8,128)(2,1)}, u32[]{:S(2)}) copy-start(bf16[1280,1280]{1,0:T(8,128)(2,1)} %param.20) | copy-start | bytes 9830404
  31.8 3.4 %copy-start.11 = (s32[16]{0:T(128)S(1)}, s32[16]{0:T(128)}, u32[]{:S(2)}) copy-start(s32[16]{0:T(128)} %param.22) | copy-start | bytes 196
  73.4 1.6 copy-start.4
  109.0 1.7 copy-start.1
  110.8 1.7 copy-start.3
  112.5 23.3 %copy-start.9 = (pred[16]{0:T(512)(128)(4,1)S(1)}, pred[16]{0:T(512)(128)(4,1)}, u32[]{:S(2)}) copy-start(pred[16]{0:T(512)(128)(4,1)} %compare_and_fusion) | copy-start | bytes 52
  131.5 10.7 %all-to-all-start = ((bf16[4,2,32,576]{3,2,1,0:T(8,128)(2,1)}), bf16[4,2,32,576]{3,2,1,0:T(8,128)(2,1)}, u32[]{:S(2)}, u32[]{:S(2)}) async-start(bf16[4,2,32,576]{3,2,1,0:T(8,128)(2,1)} %bitcast.56), calls=%async_computation | async-start | bytes 655360 | tf_op jit(solution)/shard_map/all_to_all | solution.py:194
  135.6 105.0 %all-gather.11.cloned.1.call-start = ((), (), s32[]{:S(2)}) async-start(), calls=%async_computation.5 | async-start | bytes 4866048 | tf_op jit(solution)/shard_map/all_gather | solution.py:238
  147.5 3.3 %copy-start.8 = (bf16[512,1024]{1,0:T(8,128)(2,1)S(1)}, bf16[512,1024]{1,0:T(8,128)(2,1)}, u32[]{:S(2)}) copy-start(bf16[512,1024]{1,0:T(8,128)(2,1)} %param.24) | copy-start | bytes 3145732
  148.5 2.7 %copy-start.5 = (bf16[4,5,64,1280]{3,2,1,0:T(8,128)(2,1)S(1)}, bf16[4,5,64,1280]{3,2,1,0:T(8,128)(2,1)}, u32[]{:S(2)}) copy-start(bf16[4,5,64,1280]{3,2,1,0:T(8,128)(2,1)} %copy.45) | copy-start | bytes 9830404
  148.5 2.7 %copy-start.7 = (f32[64,1280]{1,0:T(8,128)S(1)}, f32[64,1280]{1,0:T(8,128)}, u32[]{:S(2)}) copy-start(f32[64,1280]{1,0:T(8,128)} %reduce_sum.89) | copy-start | bytes 983044
Sparse Core Ops, SparseCore 0:
  9.6 31.7 all-gather.4
  43.1 30.3 all-gather.6
  75.0 33.9 all-gather.8
  179.3 61.2 all-gather.10

commit v2 on v1

--- a/solution.py
+++ b/solution.py
@@ -11,6 +11,7 @@
 
 HEAD = 64
 POOL = 4
+LANES = 128
 LOG2E = 1.4426950408889634
 
 epsilon_norm = 1e-05
@@ -27,7 +28,7 @@
         for r in range(roles)
         for s in range(shards)
     ]
-    slots = -(-int(max(counts)) // HEAD) * HEAD
+    slots = -(-int(max(counts)) // LANES) * LANES
     send = np.full((roles, shards, slots), -1, np.int32)
     where = np.zeros(total, np.int32)
     for r in range(roles):
@@ -39,9 +40,13 @@
     return send, receive.astype(np.int32)
 
 
-def teacher_kernel(valid_ref, table_ref, hidden_ref, gathered_ref, out_ref, weight, projected, attended):
+def teacher_kernel(
+    first, valid_ref, table_ref, hidden_ref, gathered_ref, out_ref,
+    held, place, weight, projected, attended, copied,
+):
     clip = pl.program_id(0)
-    width, columns = gathered_ref.shape
+    shards, width, slots = held.shape
+    columns = shards * slots
     needed = weight.shape[1]
     mine = needed // 3
     frames = hidden_ref.shape[1]
@@ -49,14 +54,25 @@
 
     @pl.when(clip == 0)
     def _():
-        place = lax.broadcasted_iota(jnp.int32, (columns, needed), 0) == table_ref[...]
-        place = place.astype(jnp.float32).astype(jnp.bfloat16)
+        copy = pltpu.make_async_copy(gathered_ref.at[:, pl.ds(first, width), :], held, copied)
+        copy.start()
+
+        @pl.loop(0, columns // LANES)
+        def _(i):
+            start = pl.multiple_of(i * LANES, LANES)
+            row = lax.broadcasted_iota(jnp.int32, (LANES, needed), 0) + start
+            place[pl.ds(start, LANES), :] = (
+                (row == table_ref[...]).astype(jnp.float32).astype(jnp.bfloat16)
+            )
+
+        copy.wait()
 
         @pl.loop(0, width // 256)
         def _(i):
             part = pl.ds(pl.multiple_of(i * 256, 256), 256)
+            joined = jnp.concatenate([held[s, part, :] for s in range(shards)], axis=1)
             weight[part, :] = jnp.dot(
-                gathered_ref[part, :], place, preferred_element_type=jnp.float32
+                joined, place[...], preferred_element_type=jnp.float32
             ).astype(jnp.bfloat16)
 
     @pl.loop(0, frames // rows)
@@ -72,14 +88,12 @@
 
     key_index = lax.broadcasted_iota(jnp.int32, (1, frames), 1)
     bias = jnp.where(key_index < valid_ref[clip], 0.0, -1e30)
-    ones = jnp.ones((frames, HEAD), jnp.bfloat16)
     scale = HEAD ** (-0.5) * LOG2E
     half = 256
     for j in range(mine // HEAD):
         lanes = slice(j * HEAD, (j + 1) * HEAD)
         keys = projected[:, mine + j * HEAD : mine + (j + 1) * HEAD]
         values = projected[:, 2 * mine + j * HEAD : 2 * mine + (j + 1) * HEAD]
-        values = jnp.concatenate([values, ones], axis=1)
         for h in range(frames // half):
             query = projected[h * half : (h + 1) * half, lanes]
             scores = lax.dot_general(
@@ -87,43 +101,48 @@
             )
             scores = scores + bias
             top = jnp.max(scores, axis=-1, keepdims=True)
-            raised = jnp.exp2((scores - top) * scale).astype(jnp.bfloat16)
-            both = jnp.dot(raised, values, preferred_element_type=jnp.float32)
-            attended[h * half : (h + 1) * half, lanes] = (
-                both[:, :HEAD] / both[:, HEAD : HEAD + 1]
+            raised = jnp.exp2((scores - top) * scale)
+            weights = raised * (1.0 / jnp.sum(raised, axis=-1, keepdims=True))
+            attended[h * half : (h + 1) * half, lanes] = jnp.dot(
+                weights.astype(jnp.bfloat16), values, preferred_element_type=jnp.float32
             ).astype(jnp.bfloat16)
 
     pooled = frames // POOL
     row = lax.broadcasted_iota(jnp.int32, (pooled, frames), 0)
     column = lax.broadcasted_iota(jnp.int32, (pooled, frames), 1)
     average = jnp.where(column // POOL == row, 1.0 / POOL, 0.0).astype(jnp.bfloat16)
-    out_ref[0] = jnp.dot(average, attended[...], preferred_element_type=jnp.float32).astype(
-        jnp.bfloat16
-    )
-
-
-def teacher(hidden, gathered, table, valid):
+    mean = jnp.dot(average, attended[...], preferred_element_type=jnp.float32)
+    high = mean.astype(jnp.bfloat16)
+    out_ref[0, :, :mine] = high
+    out_ref[0, :, mine:] = (mean - high.astype(jnp.float32)).astype(jnp.bfloat16)
+
+
+def teacher(hidden, gathered, first, table, valid):
     clips, frames, width = hidden.shape
-    columns = gathered.shape[1]
+    shards, _, slots = gathered.shape
+    columns = shards * slots
     needed = table.shape[1]
     mine = needed // 3
     return pl.pallas_call(
-        teacher_kernel,
+        functools.partial(teacher_kernel, first),
         grid=(clips,),
-        out_shape=jax.ShapeDtypeStruct((clips, frames // POOL, mine), jnp.bfloat16),
+        out_shape=jax.ShapeDtypeStruct((clips, frames // POOL, 2 * mine), jnp.bfloat16),
         in_specs=[
             pl.BlockSpec(memory_space=pltpu.SMEM),
             pl.BlockSpec((1, needed), lambda i: (0, 0)),
             pl.BlockSpec((1, frames, width), lambda i: (i, 0, 0)),
-            pl.BlockSpec((width, columns), lambda i: (0, 0)),
+            pl.BlockSpec(memory_space=pl.ANY),
         ],
-        out_specs=pl.BlockSpec((1, frames // POOL, mine), lambda i: (i, 0, 0)),
+        out_specs=pl.BlockSpec((1, frames // POOL, 2 * mine), lambda i: (i, 0, 0)),
         scratch_shapes=[
+            pltpu.VMEM((shards, width, slots), jnp.bfloat16),
+            pltpu.VMEM((columns, needed), jnp.bfloat16),
             pltpu.VMEM((width, needed), jnp.bfloat16),
             pltpu.VMEM((frames, needed), jnp.bfloat16),
             pltpu.VMEM((frames, mine), jnp.bfloat16),
+            pltpu.SemaphoreType.DMA,
         ],
-        compiler_params=pltpu.CompilerParams(vmem_limit_bytes=40 * 1024 * 1024),
+        compiler_params=pltpu.CompilerParams(vmem_limit_bytes=48 * 1024 * 1024),
         cost_estimate=pl.CostEstimate(
             flops=2 * clips * frames * needed * (width + frames),
             bytes_accessed=2 * width * (columns + clips * frames),
@@ -182,20 +201,23 @@
     whisper_width = whisper_hidden.shape[-1]
     wavlm_part, wavlm_table = my_columns(wavlm_qkv, wavlm_width)
     whisper_part, whisper_table = my_columns(whisper_qkv, whisper_width)
-    wavlm_all, whisper_all, latent_all = lax.all_gather(
-        (wavlm_part, whisper_part, latent), "dp", axis=1, tiled=True
-    )
-
-    wavlm_att = teacher(wavlm_hidden, wavlm_all, wavlm_table, valid_here)
-    whisper_att = teacher(whisper_hidden, whisper_all, whisper_table, valid_here)
+    slots = wavlm_part.shape[1]
+    parts = jnp.concatenate([wavlm_part, whisper_part, latent.reshape(-1, slots)], axis=0)
+    gathered = lax.all_gather(parts, "dp", axis=0, tiled=False)
+    latent_all = gathered[:, wavlm_width + whisper_width :, :].reshape(
+        dp_count, latent.shape[0], latent.shape[1], pooled, stu
+    ).transpose(1, 0, 2, 3, 4)
+
+    wavlm_att = teacher(wavlm_hidden, gathered, 0, wavlm_table, valid_here)
+    whisper_att = teacher(whisper_hidden, gathered, wavlm_width, whisper_table, valid_here)
     att = jnp.concatenate([wavlm_att, whisper_att], axis=-1)
     mine = att.shape[-1]
     att = att.reshape(clips_here, roles, quarter, mine).transpose(1, 0, 2, 3)
     att = lax.all_to_all(att, "role", split_axis=0, concat_axis=0, tiled=True)
     att = att.reshape(roles, clips_here * quarter, mine)
 
-    slots = jnp.arange(all_clips)
-    slot_of = jnp.sum(jnp.where(slot_clip[None, :] == slots[:, None], slots[None, :], 0), axis=1)
+    order = jnp.arange(all_clips)
+    slot_of = jnp.sum(jnp.where(slot_clip[None, :] == order[:, None], order[None, :], 0), axis=1)
     latent_by_clip = jnp.take(latent_all.reshape(all_clips, pooled, stu), slot_of, axis=0)
     latent_rows = lax.dynamic_slice(
         latent_by_clip, (column * clips_here, role * quarter, 0), (clips_here, quarter, stu)
@@ -212,8 +234,13 @@
         )
         weight = out_weight.reshape(-1, roles, HEAD, width).transpose(1, 0, 2, 3)
         weight = weight.reshape(width, width)
-        rows = att_rows.transpose(1, 0, 2).reshape(clips_here * quarter, width)
-        target = here + jnp.dot(rows, weight, preferred_element_type=jnp.float32)
+        share = width // roles
+        high, low = (
+            part.transpose(1, 0, 2).reshape(clips_here * quarter, width)
+            for part in (att_rows[:, :, :share], att_rows[:, :, share:])
+        )
+        target = jnp.dot(high, weight, preferred_element_type=jnp.float32)
+        target = here + (target + jnp.dot(low, weight, preferred_element_type=jnp.float32))
         return slope_of(latent_rows, target.astype(jnp.bfloat16), head_weight, row_mask)
 
     split = wavlm_att.shape[-1]

time: 258 us -> 275 us (1.066)
  local copies, waits for them, and re-layouts: 43.5 us -> 65.9 us
  waiting for transfers between devices: 120 us -> 110 us
  Pallas kernels: 32.8 us -> 38.1 us
    all_gather x0 -> x1, local copies, waits for them, and re-layouts: none -> 9.94 us  [per_device(): gathered = lax.all_gather(parts, 'dp', axis=0, tiled=False)]
    reshape x2 -> x8, local copies, waits for them, and re-layouts: 2.83 us -> 12.2 us  [the longest x2 5.83 us: per_device(): gathered[:, wavlm_width + whisper_width:, :]]
    pallas_call x2, Pallas kernels: 32.8 us -> 38.1 us  [teacher(): pl.pallas_call(functools.partial(teacher_kernel, first), grid=(clips,), o...]
    all_to_all x1, waiting for transfers between devices: 4.52 us -> 0.01 us  [per_device(): att = lax.all_to_all(att, 'role', split_axis=0, concat_axis=0, tiled=True)]
    all_gather x3 -> x1, waiting for transfers between devices: 53.2 us -> 49 us  [per_device(): gathered = lax.all_gather(parts, 'dp', axis=0, tiled=False)]
    slice x0 -> x1, local copies, waits for them, and re-layouts: none -> 3.21 us  [per_device(): gathered[:, wavlm_width + whisper_width:, :]]
    unnamed x27 -> x37, local copies, waits for them, and re-layouts: 11.7 us -> 8.84 us
    dot_general x2, matrix products: 4.91 us -> 2.06 us  [my_columns(): jnp.dot(shard, place.astype(jnp.bfloat16), preferred_element_type=jnp.flo...]
  transfers between devices with their start and end apart: 5 -> 3, of which waited for: 5 -> 2; matrix products, arithmetic and copies ran while one was open for 13% -> 11% of each run, Pallas kernels for 6% -> 0%
where the time goes in v2:
time: 275 us; the launch traced here: 274 us
  waiting for transfers between devices  110 us (40%)
  local copies, waits for them, and re-layouts  65.9 us (24%)
  Pallas kernels  38.1 us (14%)
  blocking collectives  19.7 us (7%)
  between operations  14.4 us (5%)
  other arithmetic  11.6 us (4%)
  matrix products  9.42 us (3%)
  starting transfers between devices  4.23 us (2%)
    all_gather x1, waiting for transfers between devices, per_device(): grad = lax.all_gather(grad, ('role', 'dp'), axis=0, tiled=True)  61.4 us
    all_gather x1, waiting for transfers between devices, per_device(): gathered = lax.all_gather(parts, 'dp', axis=0, tiled=False)  49 us
    pallas_call x2, Pallas kernels, teacher(): pl.pallas_call(functools.partial(teacher_kernel, first), grid=(clips,), o...  38.1 us
    all_to_all x1, blocking collectives, per_device(): lax.all_to_all(slope, ('role', 'dp'), split_axis=0, concat_axis=0, tiled=...  19.7 us
    all_gather x1, local copies, waits for them, and re-layouts, per_device(): gathered = lax.all_gather(parts, 'dp', axis=0, tiled=False)  9.94 us
    unnamed x37, local copies, waits for them, and re-layouts  8.84 us
    transpose x2, local copies, waits for them, and re-layouts, slope_teacher(): weight = out_weight.reshape(-1, roles, HEAD, width).transpose(1, 0, 2, 3)  7.21 us
    reshape x2, local copies, waits for them, and re-layouts, per_device(): gathered[:, wavlm_width + whisper_width:, :]  5.83 us
  transfers between devices with their start and end apart: 3, of which 2 were waited for; matrix products, arithmetic and copies ran while one was open for 11% of the time, Pallas kernels for 0%

profile of v2, /device:TPU:0, one launch (start us, length us, event | category | flops | bytes accessed | tf_op | source)
XLA Modules:
  0.0 273.8 jit_solution(4104850847991868844)
XLA Ops:
  12.6 3.3 %copy.49 = bf16[4,4,64,1024]{3,2,1,0:T(8,128)(2,1)} copy(bf16[4,4,64,1024]{3,2,0,1:T(8,128)(2,1)} %bitcast.84) | data formatting | bytes 4194304 | tf_op jit(solution)/shard_map/transpose | solution.py:235
  17.0 2.5 reshape.198
  19.7 3.9 %copy.52 = bf16[4,5,64,1280]{3,2,1,0:T(8,128)(2,1)} copy(bf16[4,5,64,1280]{3,2,0,1:T(8,128)(2,1)} %bitcast.81) | data formatting | bytes 6553600 | tf_op jit(solution)/shard_map/transpose | solution.py:235
  23.6 2.3 dynamic-slice_convert_fusion
  25.9 2.6 reshape.200
  28.5 2.6 reduce_sum.85
  31.1 2.8 %reduce_sum.89 = f32[64,1280]{1,0:T(8,128)} reduce(f32[64,4,1280]{2,1,0:T(4,128)} %reshape.200, f32[]{:T(128)} %constant.68.clone.1), dimensions={1}, to_apply=%region_5.6 | reduce | flops 245760 | bytes 1638404 | tf_op jit(solution)/shard_map/reduce_sum | solution.py:232
  35.5 49.0 %all-gather.6.cloned.1.call-done = bf16[26624,128]{0,1:T(8,128)(2,1)} async-done(((bf16[3328,128]{0,1:T(8,128)(2,1)}), bf16[26624,128]{0,1:T(8,128)(2,1)}) %all-gather.6.cloned.1.call-update) | async-done | bytes 6815760 | tf_op jit(solution)/shard_map/all_gather | solution.py:206
  84.5 9.9 %copy.45 = bf16[26624,128]{1,0:T(8,128)(2,1)} copy(bf16[26624,128]{0,1:T(8,128)(2,1)} %all-gather.6.cloned.1.call-done) | data formatting | bytes 13631488 | tf_op jit(solution)/shard_map/all_gather | solution.py:206
  94.4 3.2 %slice.36 = bf16[8,1024,128]{2,1,0:T(8,128)(2,1)} slice(bf16[8,3328,128]{2,1,0:T(8,128)(2,1)} %bitcast.72), slice={[0:8], [2304:3328], [0:128]} | slice | bytes 4194304 | tf_op jit(solution)/shard_map/slice | solution.py:207
  97.6 21.3 %shard_map.159 = bf16[2,128,640]{2,1,0:T(8,128)(2,1)S(1)} custom-call(s32[2]{0:T(128)S(1)} %get-tuple-element.17.valid_ref, s32[1,960]{1,0:T(1,128)S(1)} %constant_dynamic-slice_fusion.table_ref, bf16[2,512,1280]{2,1,0:T(8,128)(2,1)S(1)} %copy-done.2, bf16[8,3328,128]{2,1,0:T(8,128)(2,1)} %bitcast.73), custom_call_target="tpu_custom_call" | custom-call | flops 3523215360 | bytes 5242880 | tf_op jit(solution)/shard_map/pallas_call | solution.py:126
  118.9 16.8 %shard_map.158 = bf16[2,128,512]{2,1,0:T(8,128)(2,1)S(1)} custom-call(s32[2]{0:T(128)S(1)} %get-tuple-element.17.valid_ref, s32[1,768]{1,0:T(1,128)S(1)} %constant_dynamic-slice_fusion.1.table_ref, bf16[2,512,1024]{2,1,0:T(8,128)(2,1)S(1)} %copy-done.1, bf16[8,3328,128]{2,1,0:T(8,128)(2,1)} %bitcast.74), custom_call_target="tpu_custom_call" | custom-call | flops 2415919104 | bytes 4194304 | tf_op jit(solution)/shard_map/pallas_call | solution.py:126
  136.6 4.2 %all-to-all-start = ((bf16[4,2,32,1152]{3,2,1,0:T(8,128)(2,1)}), bf16[4,2,32,1152]{3,2,1,0:T(8,128)(2,1)}, u32[]{:S(2)}, u32[]{:S(2)}) async-start(bf16[4,2,32,1152]{3,2,1,0:T(8,128)(2,1)} %bitcast.82), calls=%async_computation | async-start | bytes 1179648 | tf_op jit(solution)/shard_map/all_to_all | solution.py:216
  140.9 2.7 reshape.177
  143.6 3.1 %copy.46 = bf16[8,2,1,128,512]{4,3,0,1,2:T(8,128)(2,1)} copy(bf16[8,2,1,128,512]{4,3,1,0,2:T(8,128)(2,1)} %reshape.177) | data formatting | bytes 4194304 | tf_op jit(solution)/shard_map/reshape | solution.py:207
  146.7 2.3 gather_fusion
  151.7 1.8 slice_bitcast_fusion.2
  155.7 1.8 reshape.190
  162.6 2.7 fusion.16
  169.9 3.1 %reshape.194 = bf16[64,32,72]{2,1,0:T(8,128)(2,1)} reshape(bf16[64,2304]{1,0:T(8,128)(2,1)} %pad_maximum_fusion.2) | data formatting | bytes 589824 | tf_op jit(solution)/shard_map/reshape | solution.py:255
  174.2 19.7 %all_to_all.10 = bf16[32,64,72]{2,1,0:T(8,128)(2,1)S(1)} all-to-all(bf16[32,64,72]{2,1,0:T(8,128)(2,1)S(1)} %bitcast.85), channel_id=1, replica_groups=mesh['role'=4,'dp'=8] {'role','dp'}, dimensions={0} | all-to-all | bytes 589824 | tf_op jit(solution)/shard_map/all_to_all | solution.py:256
  195.2 61.4 %all-gather.4.cloned.1.call-done = f32[2304,512]{1,0:T(8,128)} async-done(((f32[72,512]{1,0:T(8,128)}), f32[2304,512]{1,0:T(8,128)}) %all-gather.4.cloned.1.call-update) | async-done | bytes 4718608 | tf_op jit(solution)/shard_map/all_gather | solution.py:265
  256.6 3.5 %slice_bitcast_fusion = f32[512,1280]{0,1:T(8,128)} fusion(f32[2304,512]{1,0:T(8,128)} %all-gather.4.cloned.1.call-done), kind=kLoop, calls=%fused_computation.1 | loop fusion | bytes 5242880 | tf_op jit(solution)/shard_map/transpose | solution.py:266
  260.1 3.2 %copy.57 = f32[512,1280]{1,0:T(8,128)} copy(f32[512,1280]{0,1:T(8,128)} %slice_bitcast_fusion) | data formatting | bytes 5242880
  (81 shorter events, 29.7 us)
Async XLA Ops:
  7.2 161.0 %copy-start = (bf16[512,1280]{1,0:T(8,128)(2,1)S(1)}, bf16[512,1280]{1,0:T(8,128)(2,1)}, u32[]{:S(2)}) copy-start(bf16[512,1280]{1,0:T(8,128)(2,1)} %param.25) | copy-start | bytes 3932164
  7.2 3.9 %copy-start.11 = (bf16[1024,384]{1,0:T(8,128)(2,1)S(1)}, bf16[1024,384]{1,0:T(8,128)(2,1)}, u32[]{:S(2)}) copy-start(bf16[1024,384]{1,0:T(8,128)(2,1)} %param.17) | copy-start | bytes 2359300
  7.2 77.3 %all-gather.6.cloned.1.call-start = ((), (), s32[]{:S(2)}) async-start(), calls=%async_computation.3 | async-start | bytes 7667712 | tf_op jit(solution)/shard_map/all_gather | solution.py:206
  12.5 3.3 %copy-start.1 = (bf16[2,512,1024]{2,1,0:T(8,128)(2,1)S(1)}, bf16[2,512,1024]{2,1,0:T(8,128)(2,1)}, u32[]{:S(2)}) copy-start(bf16[2,512,1024]{2,1,0:T(8,128)(2,1)} %hidden_ref.2) | copy-start | bytes 6291460
  15.9 3.6 %copy-start.15 = (s32[16]{0:T(128)S(1)}, s32[16]{0:T(128)}, u32[]{:S(2)}) copy-start(s32[16]{0:T(128)} %param.21) | copy-start | bytes 196
  28.5 6.9 %copy-start.16 = (s32[16]{0:T(128)S(1)}, s32[16]{0:T(128)}, u32[]{:S(2)}) copy-start(s32[16]{0:T(128)} %param.22) | copy-start | bytes 196
  94.4 3.2 %copy-start.2 = (bf16[2,512,1280]{2,1,0:T(8,128)(2,1)S(1)}, bf16[2,512,1280]{2,1,0:T(8,128)(2,1)}, u32[]{:S(2)}) copy-start(bf16[2,512,1280]{2,1,0:T(8,128)(2,1)} %hidden_ref.3) | copy-start | bytes 7864324
  135.7 5.2 %copy-start.7 = (bf16[8,1024,128]{2,1,0:T(8,128)(2,1)S(1)}, bf16[8,1024,128]{2,1,0:T(8,128)(2,1)}, u32[]{:S(2)}) copy-start(bf16[8,1024,128]{2,1,0:T(8,128)(2,1)} %slice.36) | copy-start | bytes 6291460
  136.6 13.9 %all-to-all-start = ((bf16[4,2,32,1152]{3,2,1,0:T(8,128)(2,1)}), bf16[4,2,32,1152]{3,2,1,0:T(8,128)(2,1)}, u32[]{:S(2)}, u32[]{:S(2)}) async-start(bf16[4,2,32,1152]{3,2,1,0:T(8,128)(2,1)} %bitcast.82), calls=%async_computation | async-start | bytes 1179648 | tf_op jit(solution)/shard_map/all_to_all | solution.py:216
  140.8 115.8 %all-gather.4.cloned.1.call-start = ((), (), s32[]{:S(2)}) async-start(), calls=%async_computation.2 | async-start | bytes 4866048 | tf_op jit(solution)/shard_map/all_gather | solution.py:265
  149.2 1.3 copy-start.5
  150.6 10.5 %copy-start.4 = (bf16[4,4,64,1024]{3,2,1,0:T(8,128)(2,1)S(1)}, bf16[4,4,64,1024]{3,2,1,0:T(8,128)(2,1)}, u32[]{:S(2)}) copy-start(bf16[4,4,64,1024]{3,2,1,0:T(8,128)(2,1)} %copy.49) | copy-start | bytes 6291460
  161.1 1.5 copy-start.13
  162.5 2.7 copy-start.9
  162.5 2.7 copy-start.14
  162.5 4.4 %copy-start.12 = (bf16[64,1280]{1,0:T(8,128)(2,1)S(1)}, bf16[64,1280]{1,0:T(8,128)(2,1)}, u32[]{:S(2)}) copy-start(bf16[64,1280]{1,0:T(8,128)(2,1)} %reshape.193) | copy-start | bytes 491524
  165.2 1.2 copy-start.10
  165.3 2.2 copy-start.3
  165.3 2.2 copy-start.8
  169.9 24.1 %copy-start.6 = (bf16[16,128,512]{2,1,0:T(8,128)(2,1)S(1)}, bf16[16,128,512]{2,1,0:T(8,128)(2,1)}, u32[]{:S(2)}) copy-start(bf16[16,128,512]{2,1,0:T(8,128)(2,1)} %copy-done.5) | copy-start | bytes 6291460
Sparse Core Ops, SparseCore 0:
  12.7 71.7 all-gather.5
  195.3 61.2 all-gather.3

commit v3 on v2

--- a/solution.py
+++ b/solution.py
@@ -151,9 +151,56 @@
     )(valid, table, hidden, gathered)
 
 
+def pick_kernel(*refs):
+    out_ref = refs[-1]
+    first = 0
+    for shard_ref, table_ref in zip(refs[:-1:2], refs[1:-1:2]):
+        depth, columns = shard_ref.shape
+        row = lax.broadcasted_iota(jnp.int32, (columns, out_ref.shape[1]), 0)
+        place = (row == table_ref[...]).astype(jnp.float32).astype(jnp.bfloat16)
+        out_ref[first : first + depth, :] = jnp.dot(
+            shard_ref[...], place, preferred_element_type=jnp.float32
+        ).astype(jnp.bfloat16)
+        first += depth
+
+
+def pick(pairs):
+    depth = sum(shard.shape[0] for shard, _ in pairs)
+    slots = pairs[0][1].shape[1]
+    operands = [array for pair in pairs for array in pair]
+    return pl.pallas_call(
+        pick_kernel,
+        out_shape=jax.ShapeDtypeStruct((depth, slots), jnp.bfloat16),
+        in_specs=[pl.BlockSpec(memory_space=pltpu.VMEM)] * len(operands),
+        out_specs=pl.BlockSpec(memory_space=pltpu.VMEM),
+        compiler_params=pltpu.CompilerParams(vmem_limit_bytes=24 * 1024 * 1024),
+    )(*operands)
+
+
+def finish_kernel(blocks_ref, *out_refs):
+    first = 0
+    for out_ref in out_refs:
+        width = out_ref.shape[1]
+        for start in range(0, width, LANES):
+            part = blocks_ref[first + start : first + start + LANES, :].astype(jnp.float32)
+            out_ref[:, start : start + LANES] = part.T
+        first += width
+
+
+def finish(blocks, widths):
+    depth = blocks.shape[1]
+    return pl.pallas_call(
+        finish_kernel,
+        out_shape=[jax.ShapeDtypeStruct((depth, width), jnp.float32) for width in widths],
+        in_specs=[pl.BlockSpec(memory_space=pltpu.VMEM)],
+        out_specs=[pl.BlockSpec(memory_space=pltpu.VMEM)] * len(widths),
+        compiler_params=pltpu.CompilerParams(vmem_limit_bytes=32 * 1024 * 1024),
+    )(blocks)
+
+
 def slope_of(latent_rows, target, head_weight, row_mask):
     predicted = jnp.dot(latent_rows, head_weight, preferred_element_type=jnp.float32)
-    target_f = target.astype(jnp.float32)
+    target_f = lax.reduce_precision(target, 8, 7)
     width_scale = 1.0 / target.shape[-1]
     pred_norm = jnp.sqrt(jnp.sum(predicted * predicted, axis=-1) + epsilon_cos)
     target_norm = jnp.sqrt(jnp.sum(target_f * target_f, axis=-1) + epsilon_cos)
@@ -193,23 +240,23 @@
     def my_columns(shard, width):
         send, receive = column_tables(width, dp_count, roles)
         wanted = jnp.asarray(send)[role, column]
-        place = jnp.arange(shard.shape[1])[:, None] == wanted[None, :]
-        picked = jnp.dot(shard, place.astype(jnp.bfloat16), preferred_element_type=jnp.float32)
-        return picked.astype(jnp.bfloat16), jnp.asarray(receive)[role][None, :]
+        return wanted[None, :], jnp.asarray(receive)[role][None, :]
 
     wavlm_width = wavlm_hidden.shape[-1]
     whisper_width = whisper_hidden.shape[-1]
-    wavlm_part, wavlm_table = my_columns(wavlm_qkv, wavlm_width)
-    whisper_part, whisper_table = my_columns(whisper_qkv, whisper_width)
-    slots = wavlm_part.shape[1]
-    parts = jnp.concatenate([wavlm_part, whisper_part, latent.reshape(-1, slots)], axis=0)
-    gathered = lax.all_gather(parts, "dp", axis=0, tiled=False)
-    latent_all = gathered[:, wavlm_width + whisper_width :, :].reshape(
-        dp_count, latent.shape[0], latent.shape[1], pooled, stu
-    ).transpose(1, 0, 2, 3, 4)
+    wavlm_wanted, wavlm_table = my_columns(wavlm_qkv, wavlm_width)
+    whisper_wanted, whisper_table = my_columns(whisper_qkv, whisper_width)
+    parts = pick([(wavlm_qkv, wavlm_wanted), (whisper_qkv, whisper_wanted)])
+    gathered = lax.all_gather(parts, "dp", axis=0, tiled=True)
+    gathered, latent = lax.optimization_barrier((gathered, latent))
+    latent_all = lax.all_gather(latent.reshape(-1, stu), "dp", axis=0, tiled=True)
+    gathered = gathered.reshape(dp_count, wavlm_width + whisper_width, -1)
 
     wavlm_att = teacher(wavlm_hidden, gathered, 0, wavlm_table, valid_here)
     whisper_att = teacher(whisper_hidden, gathered, wavlm_width, whisper_table, valid_here)
+    wavlm_att, whisper_att, latent_all = lax.optimization_barrier(
+        (wavlm_att, whisper_att, latent_all)
+    )
     att = jnp.concatenate([wavlm_att, whisper_att], axis=-1)
     mine = att.shape[-1]
     att = att.reshape(clips_here, roles, quarter, mine).transpose(1, 0, 2, 3)
@@ -218,7 +265,10 @@
 
     order = jnp.arange(all_clips)
     slot_of = jnp.sum(jnp.where(slot_clip[None, :] == order[:, None], order[None, :], 0), axis=1)
-    latent_by_clip = jnp.take(latent_all.reshape(all_clips, pooled, stu), slot_of, axis=0)
+    halves, owned = latent.shape[:2]
+    half, rest = slot_of // (dp_count * owned), slot_of % (dp_count * owned)
+    place = (rest // owned * halves + half) * owned + rest % owned
+    latent_by_clip = jnp.take(latent_all.reshape(all_clips, pooled, stu), place, axis=0)
     latent_rows = lax.dynamic_slice(
         latent_by_clip, (column * clips_here, role * quarter, 0), (clips_here, quarter, stu)
     ).reshape(clips_here * quarter, stu)
@@ -241,7 +291,7 @@
         )
         target = jnp.dot(high, weight, preferred_element_type=jnp.float32)
         target = here + (target + jnp.dot(low, weight, preferred_element_type=jnp.float32))
-        return slope_of(latent_rows, target.astype(jnp.bfloat16), head_weight, row_mask)
+        return slope_of(latent_rows, target, head_weight, row_mask)
 
     split = wavlm_att.shape[-1]
     slope = jnp.concatenate(
@@ -262,8 +312,8 @@
         (((0,), (0,)), ((), ())),
         preferred_element_type=jnp.float32,
     )
-    grad = lax.all_gather(grad, ("role", "dp"), axis=0, tiled=True)
-    return grad[:wavlm_width].T, grad[wavlm_width:].T
+    grad = lax.all_gather(grad.astype(jnp.bfloat16), ("role", "dp"), axis=0, tiled=True)
+    return tuple(finish(grad, (wavlm_width, whisper_width)))
 
 
 def solution(mesh):

time: 275 us -> 251 us (0.913)
  local copies, waits for them, and re-layouts: 65.9 us -> 38.6 us
  waiting for transfers between devices: 110 us -> 115 us
  Pallas kernels: 38.1 us -> 42.7 us
    all_gather x1 -> x0, local copies, waits for them, and re-layouts: 9.94 us -> none  [per_device(): gathered = lax.all_gather(parts, 'dp', axis=0, tiled=False)]
    reshape x4 -> x0, local copies, waits for them, and re-layouts: 7.23 us -> none  [the longest x2 5.83 us: per_device(): gathered[:, wavlm_width + whisper_width:, :]]
    all_to_all x1, waiting for transfers between devices: 0.01 us -> 5.34 us  [per_device(): att = lax.all_to_all(att, 'role', split_axis=0, concat_axis=0, tiled=True)]
    transpose x2 -> x0, local copies, waits for them, and re-layouts: 5.26 us -> none  [per_device(): return (grad[:wavlm_width].T, grad[wavlm_width:].T)]
    pallas_call x0 -> x2, Pallas kernels: none -> 4.34 us  [the longest x1 2.82 us: finish(): pl.pallas_call(finish_kernel, out_shape=[jax.ShapeDtypeStruct((depth, wid...]
    slice x1 -> x0, local copies, waits for them, and re-layouts: 3.21 us -> none  [per_device(): gathered[:, wavlm_width + whisper_width:, :]]
    all_gather x2 -> x3, waiting for transfers between devices: 110 us -> 110 us  [the longest x1 55.2 us: per_device(): lax.all_gather(grad.astype(jnp.bfloat16), ('role', 'dp'), axis=0, tiled=T...]
    unnamed x37 -> x38, local copies, waits for them, and re-layouts: 8.84 us -> 9.41 us
  transfers between devices with their start and end apart: 3 -> 4, of which waited for: 2 -> 3; matrix products, arithmetic and copies ran while one was open for 11% -> 8% of each run, Pallas kernels for 0% -> 15%
where the time goes in v3:
time: 251 us; the launch traced here: 250 us
  waiting for transfers between devices  115 us (46%)
  Pallas kernels  42.7 us (17%)
  local copies, waits for them, and re-layouts  38.6 us (15%)
  blocking collectives  18.6 us (7%)
  between operations  14.1 us (6%)
  other arithmetic  9.36 us (4%)
  matrix products  7.34 us (3%)
  starting transfers between devices  4.45 us (2%)
    all_gather x1, waiting for transfers between devices, per_device(): lax.all_gather(grad.astype(jnp.bfloat16), ('role', 'dp'), axis=0, tiled=T...  55.2 us
    all_gather x1, waiting for transfers between devices, per_device(): gathered = lax.all_gather(parts, 'dp', axis=0, tiled=True)  54.5 us
    pallas_call x2, Pallas kernels, teacher(): pl.pallas_call(functools.partial(teacher_kernel, first), grid=(clips,), o...  38.3 us
    all_to_all x1, blocking collectives, per_device(): lax.all_to_all(slope, ('role', 'dp'), split_axis=0, concat_axis=0, tiled=...  18.6 us
    unnamed x38, local copies, waits for them, and re-layouts  9.41 us
    reshape x4, local copies, waits for them, and re-layouts, slope_teacher(): part.transpose(1, 0, 2).reshape(clips_here * quarter, width)  6.79 us
    all_to_all x1, waiting for transfers between devices, per_device(): att = lax.all_to_all(att, 'role', split_axis=0, concat_axis=0, tiled=True)  5.34 us
    transpose x2, local copies, waits for them, and re-layouts, slope_teacher(): weight = out_weight.reshape(-1, roles, HEAD, width).transpose(1, 0, 2, 3)  5.3 us
  transfers between devices with their start and end apart: 4, of which 3 were waited for; matrix products, arithmetic and copies ran while one was open for 8% of the time, Pallas kernels for 15%

profile of v3, /device:TPU:0, one launch (start us, length us, event | category | flops | bytes accessed | tf_op | source)
XLA Modules:
  0.0 250.3 jit_solution(17261724233288196630)
XLA Ops:
  7.2 1.7 copy.34.refs_2_
  11.3 54.5 %all-gather.4.cloned.1.call-done = bf16[18432,128]{1,0:T(8,128)(2,1)} async-done(((bf16[2304,128]{1,0:T(8,128)(2,1)}), bf16[18432,128]{1,0:T(8,128)(2,1)}) %all-gather.4.cloned.1.call-update) | async-done | bytes 4718608 | tf_op jit(solution)/shard_map/all_gather | solution.py:250
  68.5 2.2 dynamic-slice_convert_fusion
  70.8 1.7 reshape.270
  72.5 2.6 %reduce_sum.85 = f32[64,1024]{1,0:T(8,128)} reduce(f32[64,4,1024]{2,1,0:T(4,128)} %reshape.268, f32[]{:T(128)} %constant.114.clone.1), dimensions={1}, to_apply=%region_1.2 | reduce | flops 196608 | bytes 1310724 | tf_op jit(solution)/shard_map/reduce_sum | solution.py:282
  76.6 3.3 %copy.37 = bf16[4,4,64,1024]{3,2,1,0:T(8,128)(2,1)} copy(bf16[4,4,64,1024]{3,2,0,1:T(8,128)(2,1)} %bitcast.79) | data formatting | bytes 4194304 | tf_op jit(solution)/shard_map/transpose | solution.py:285
  79.9 2.0 copy.40
  83.5 1.6 copy-done.4
  85.2 17.1 %shard_map.159 = bf16[2,128,512]{2,1,0:T(8,128)(2,1)S(1)} custom-call(s32[2]{0:T(128)S(1)} %get-tuple-element.19.valid_ref, s32[1,768]{1,0:T(1,128)S(1)} %constant_dynamic-slice_fusion.4.table_ref, bf16[2,512,1024]{2,1,0:T(8,128)(2,1)S(1)} %copy-done.4, bf16[8,2304,128]{2,1,0:T(8,128)(2,1)} %bitcast.89), custom_call_target="tpu_custom_call" | custom-call | flops 2415919104 | bytes 4194304 | tf_op jit(solution)/shard_map/pallas_call | solution.py:126
  102.2 21.3 %shard_map.160 = bf16[2,128,640]{2,1,0:T(8,128)(2,1)S(1)} custom-call(s32[2]{0:T(128)S(1)} %get-tuple-element.19.valid_ref, s32[1,960]{1,0:T(1,128)S(1)} %constant_dynamic-slice_fusion.1.table_ref, bf16[2,512,1280]{2,1,0:T(8,128)(2,1)S(1)} %copy-done.3, bf16[8,2304,128]{2,1,0:T(8,128)(2,1)} %bitcast.90), custom_call_target="tpu_custom_call" | custom-call | flops 3523215360 | bytes 5242880 | tf_op jit(solution)/shard_map/pallas_call | solution.py:126
  124.5 4.1 %all-to-all-start = ((bf16[4,2,32,1152]{3,2,1,0:T(8,128)(2,1)}), bf16[4,2,32,1152]{3,2,1,0:T(8,128)(2,1)}, u32[]{:S(2)}, u32[]{:S(2)}) async-start(bf16[4,2,32,1152]{3,2,1,0:T(8,128)(2,1)} %bitcast.70), calls=%async_computation | async-start | bytes 1179648 | tf_op jit(solution)/shard_map/all_to_all | solution.py:263
  128.9 2.3 gather_fusion
  132.8 5.3 %all-to-all-done = bf16[4,2,32,1152]{3,2,1,0:T(8,128)(2,1)} async-done(((bf16[4,2,32,1152]{3,2,1,0:T(8,128)(2,1)}), bf16[4,2,32,1152]{3,2,1,0:T(8,128)(2,1)}, u32[]{:S(2)}, u32[]{:S(2)}) %all-to-all-start) | async-done | bytes 589856 | tf_op jit(solution)/shard_map/all_to_all | solution.py:263
  138.1 1.7 slice_bitcast_fusion.2
  139.8 1.8 slice_bitcast_fusion
  142.5 1.8 reshape.263
  147.4 1.8 copy.39
  149.2 1.8 reshape.260
  152.5 2.7 %fusion.12 = f32[64,1280]{1,0:T(8,128)S(1)} fusion(bf16[64,1280]{1,0:T(8,128)(2,1)S(1)} %copy-done.14, bf16[1280,1280]{1,0:T(8,128)(2,1)} %bitcast.72), kind=kOutput, calls=%fused_computation.69 | convolution fusion | flops 209715200 | bytes 3768320 | tf_op jit(solution)/shard_map/dot_general | solution.py:292
  159.9 3.1 %reshape.264 = bf16[64,32,72]{2,1,0:T(8,128)(2,1)} reshape(bf16[64,2304]{1,0:T(8,128)(2,1)} %pad_maximum_fusion.1) | data formatting | bytes 589824 | tf_op jit(solution)/shard_map/reshape | solution.py:305
  164.2 18.6 %all_to_all.10 = bf16[32,64,72]{2,1,0:T(8,128)(2,1)S(1)} all-to-all(bf16[32,64,72]{2,1,0:T(8,128)(2,1)S(1)} %bitcast.81), channel_id=1, replica_groups=mesh['role'=4,'dp'=8] {'role','dp'}, dimensions={0} | all-to-all | bytes 589824 | tf_op jit(solution)/shard_map/all_to_all | solution.py:306
  184.0 55.2 %all-gather.8.cloned.1.call-done.blocks_ref = bf16[2304,512]{1,0:T(8,128)(2,1)} async-done(((bf16[72,512]{1,0:T(8,128)(2,1)}), bf16[2304,512]{1,0:T(8,128)(2,1)}) %all-gather.8.cloned.1.call-update) | async-done | bytes 2359312 | tf_op jit(solution)/shard_map/all_gather | solution.py:315
  239.3 1.7 copy-done.1
  240.9 2.8 %shard_map.161 = (f32[512,1024]{1,0:T(8,128)}, f32[512,1280]{1,0:T(8,128)}) custom-call(bf16[2304,512]{1,0:T(8,128)(2,1)S(1)} %copy-done.1), custom_call_target="tpu_custom_call" | custom-call | tf_op jit(solution)/shard_map/pallas_call | solution.py:192
  (76 shorter events, 23.4 us)
Async XLA Ops:
  7.2 151.0 %copy-start = (bf16[512,1280]{1,0:T(8,128)(2,1)S(1)}, bf16[512,1280]{1,0:T(8,128)(2,1)}, u32[]{:S(2)}) copy-start(bf16[512,1280]{1,0:T(8,128)(2,1)} %param.25) | copy-start | bytes 3932164
  7.2 2.5 %copy-start.2 = (bf16[1024,384]{1,0:T(8,128)(2,1)S(1)}, bf16[1024,384]{1,0:T(8,128)(2,1)}, u32[]{:S(2)}) copy-start(bf16[1024,384]{1,0:T(8,128)(2,1)} %refs_0_.1) | copy-start | bytes 2359300
  7.2 58.6 %all-gather.4.cloned.1.call-start = ((), (), s32[]{:S(2)}) async-start(), calls=%async_computation.2 | async-start | bytes 5308416 | tf_op jit(solution)/shard_map/all_gather | solution.py:250
  9.0 56.9 %copy-start.16 = (s32[16]{0:T(128)S(1)}, s32[16]{0:T(128)}, u32[]{:S(2)}) copy-start(s32[16]{0:T(128)} %param.21) | copy-start | bytes 196
  11.2 112.3 %all-gather.6.cloned.1.call-start = ((), (), s32[]{:S(2)}) async-start(), calls=%async_computation.3 | async-start | bytes 2359296 | tf_op jit(solution)/shard_map/all_gather | solution.py:252
  76.6 3.3 %copy-start.9 = (bf16[1280,1280]{1,0:T(8,128)(2,1)S(1)}, bf16[1280,1280]{1,0:T(8,128)(2,1)}, u32[]{:S(2)}) copy-start(bf16[1280,1280]{1,0:T(8,128)(2,1)} %param.20) | copy-start | bytes 9830404
  79.9 3.4 %copy-start.17 = (s32[16]{0:T(128)S(1)}, s32[16]{0:T(128)}, u32[]{:S(2)}) copy-start(s32[16]{0:T(128)} %param.22) | copy-start | bytes 196
  83.5 1.6 copy-start.4
  85.2 17.1 %copy-start.3 = (bf16[2,512,1280]{2,1,0:T(8,128)(2,1)S(1)}, bf16[2,512,1280]{2,1,0:T(8,128)(2,1)}, u32[]{:S(2)}) copy-start(bf16[2,512,1280]{2,1,0:T(8,128)(2,1)} %hidden_ref.3) | copy-start | bytes 7864324
  124.5 13.6 %all-to-all-start = ((bf16[4,2,32,1152]{3,2,1,0:T(8,128)(2,1)}), bf16[4,2,32,1152]{3,2,1,0:T(8,128)(2,1)}, u32[]{:S(2)}, u32[]{:S(2)}) async-start(bf16[4,2,32,1152]{3,2,1,0:T(8,128)(2,1)} %bitcast.70), calls=%async_computation | async-start | bytes 1179648 | tf_op jit(solution)/shard_map/all_to_all | solution.py:263
  128.7 110.6 %all-gather.8.cloned.1.call-start = ((), (), s32[]{:S(2)}) async-start(), calls=%async_computation.4 | async-start | bytes 2433024 | tf_op jit(solution)/shard_map/all_gather | solution.py:315
  131.4 1.3 copy-start.7
  132.8 18.3 %copy-start.6 = (bf16[4,4,64,1024]{3,2,1,0:T(8,128)(2,1)S(1)}, bf16[4,4,64,1024]{3,2,1,0:T(8,128)(2,1)}, u32[]{:S(2)}) copy-start(bf16[4,4,64,1024]{3,2,1,0:T(8,128)(2,1)} %copy.37) | copy-start | bytes 6291460
  151.1 1.5 copy-start.14
  152.5 2.7 %copy-start.11 = (f32[64,1024]{1,0:T(8,128)S(1)}, f32[64,1024]{1,0:T(8,128)}, u32[]{:S(2)}) copy-start(f32[64,1024]{1,0:T(8,128)} %reduce_sum.85) | copy-start | bytes 786436
  152.5 2.7 %copy-start.15 = (bf16[4,8,8,256]{3,2,0,1:T(8,128)(2,1)S(1)}, bf16[4,8,8,256]{3,2,0,1:T(8,128)(2,1)}, u32[]{:S(2)}) copy-start(bf16[4,8,8,256]{3,2,0,1:T(8,128)(2,1)} %copy.45) | copy-start | bytes 393220
  152.5 4.4 %copy-start.13 = (bf16[64,1280]{1,0:T(8,128)(2,1)S(1)}, bf16[64,1280]{1,0:T(8,128)(2,1)}, u32[]{:S(2)}) copy-start(bf16[64,1280]{1,0:T(8,128)(2,1)} %reshape.263) | copy-start | bytes 491524
  155.2 1.2 copy-start.12
  155.2 2.2 copy-start.5
  155.2 2.2 copy-start.10
  159.9 23.0 %copy-start.8 = (bf16[16,128,512]{2,1,0:T(8,128)(2,1)S(1)}, bf16[16,128,512]{2,1,0:T(8,128)(2,1)}, u32[]{:S(2)}) copy-start(bf16[16,128,512]{2,1,0:T(8,128)(2,1)} %copy-done.7) | copy-start | bytes 6291460
  239.3 1.7 copy-start.1
Sparse Core Ops, SparseCore 0:
  11.4 54.3 all-gather.3
  67.4 27.9 all-gather.5
  184.2 55.0 all-gather.7
